TPU v7x, 512 devices: a whole 4x4x16 slice. The times are simulated.
512 devices in a mesh: seg: 8 (over x, core), sec: 64 (over z, y).
Axes of the slice: x: 4, y: 4, z: 16, core: 2. Of those that a mesh axis runs over, the one named last changes fastest.
Arguments:
- site_tensors: bfloat16 [8, 64, 4, 128, 128], P('seg', 'sec'), may hold values from -0.5 to 0.5
- boundary: bfloat16 [8, 64, 24, 128, 128], P('seg', 'sec'), may hold values from -6 to 6
- couplings: float32 [8, 4, 24, 24], P('seg'), may hold values from -0.9 to 0.9
- pattern: int32 [24, 24], replicated, may hold values 0 or 1
- block_sizes: int32 [64], replicated, may hold values from 64 to 128, as said below
Outputs:
- environments: bfloat16 [8, 64, 24, 128, 128], P('seg', 'sec')
- handoff: bfloat16 [8, 64, 24, 128, 128], P('seg', 'sec')
Inputs may be any that keep to these rules, and one draw needn't show every extreme that they name: `block_sizes`: each sector has between half and all of 128 live rows, and some sector has all 128.
All inputs are finite; a program needn't handle non-finite values.
Results may differ from a plain program's by a relative error of at most 0.0049.
Values may be sent and summed in bfloat16 or wider, within the bound.
No kernel may reach another device: no remote copies, remote signals or barrier semaphores. Data moves between devices by JAX's collectives and lax.ppermute only.
A program may use at most 64 MiB of HBM per device.

v0:
```python
import jax
import jax.numpy as jnp
from jax import lax
from jax.sharding import PartitionSpec as P

STATES = 4
CHARGES = 8


def passed_along(shard, axis, by):
    devices = lax.axis_size(axis)
    pairs = [(i, i + by) for i in range(devices) if 0 <= i + by < devices]
    return lax.ppermute(shard, axis, pairs)


def lookup(sizes_table, positions):
    matches = jnp.arange(sizes_table.shape[0])[None, :] == positions[:, None]
    return jnp.sum(jnp.where(matches, sizes_table[None, :], 0), axis=1)


def mask_blocks(blocks, sizes_rows, sizes_cols):
    row_index = jnp.arange(blocks.shape[-1])
    kept_mask = (row_index[None, :, None] < sizes_rows[:, None, None]) & (
        row_index[None, None, :] < sizes_cols[:, None, None]
    )
    return blocks * kept_mask.astype(jnp.bfloat16)


def finish(halfway, blocks, mixing, usable):
    sandwich = jnp.einsum("ski,sbkl->sbil", blocks, halfway, preferred_element_type=jnp.float32)
    contribution = jnp.einsum("sbc,sbil->scil", mixing, sandwich, precision=lax.Precision.HIGHEST)
    return contribution * usable.astype(jnp.float32)[:, None, None, None]


def per_device(site_tensors, boundary, couplings, pattern, block_sizes):
    sectors = block_sizes.shape[0]
    sector = lax.axis_index("sec")
    down_charge = sector % CHARGES
    state_index = jnp.arange(STATES)
    down_counts = state_index % 2
    offsets = state_index // 2 * CHARGES + down_counts
    own_size = jnp.broadcast_to(lookup(block_sizes, jnp.reshape(sector, (1,))), (STATES,))
    pattern_real = pattern.astype(jnp.float32)
    current = boundary[0, 0]
    tensors = site_tensors[0, 0]
    mixing = couplings[0] * pattern_real[None]
    target = sector + offsets
    usable = (target < sectors) & (down_charge + down_counts < CHARGES)
    target_sizes = lookup(block_sizes, jnp.minimum(target, sectors - 1))
    blocks = mask_blocks(tensors, own_size, target_sizes)
    halfway = jnp.einsum(
        "bik,skl->sbil", current, blocks, preferred_element_type=jnp.float32
    ).astype(jnp.bfloat16)
    contribution = finish(halfway, blocks, mixing, usable)
    accumulated = contribution[0] + passed_along(contribution[1], "sec", 1)
    accumulated = accumulated + passed_along(contribution[2], "sec", CHARGES)
    accumulated = accumulated + passed_along(contribution[3], "sec", CHARGES + 1)
    current = accumulated.astype(jnp.bfloat16)
    results = [current]
    handed = passed_along(current, "seg", 1)
    return (jnp.stack(results)[:, None], handed[None, None])


def solution(mesh):
    return jax.shard_map(
        per_device,
        mesh=mesh,
        in_specs=(
            P("seg", "sec", None, None, None),
            P("seg", "sec", None, None, None),
            P("seg", None, None, None),
            P(),
            P(),
        ),
        out_specs=(P("seg", "sec", None, None, None), P("seg", "sec", None, None, None)),
        check_vma=False,
    )
```

profile of v0, /device:TPU:316, one launch (start us, length us, event | category | flops | bytes accessed | tf_op | source)
XLA Modules:
  0.0 248.6 jit_solution(11671613768200634458)
XLA Ops:
  0.6 0.0 copy-start
  0.6 0.0 copy-start.1
  0.7 1.4 fusion.29
  2.0 0.6 iota_compare_fusion.2
  2.7 0.8 select_reduce_fusion
  3.6 0.1 iota_compare_fusion.1
  3.6 0.7 convert_element_type.20
  4.4 0.0 copy-done
  4.4 2.0 fusion.11
  6.4 0.0 copy-done.1
  6.4 5.3 %fusion.3 = f32[4,24,128,128]{3,1,2,0:T(8,128)} fusion(bf16[4,128,24,128]{3,1,2,0:T(8,128)(2,1)S(1)} %fusion.11, bf16[1,1,4,128,128]{4,3,2,1,0:T(8,128)(2,1)S(1)} %copy-done.1, pred[4,128]{1,0:T(4,128)(4,1)S(1)} %iota_compare_fusion.1, pred[128]{0:T(512)(128)(4,1)S(1)} %iota_compare_fusion.2), kind=kOutput, calls=%fused_computation.4 | convolution fusion | flops 402784256 | bytes 9568896 | tf_op jit(solution)/shard_map/ski,sbkl->sbil/dot_general | solution.py:30
  11.7 0.0 copy-start.2
  11.7 6.5 %copy.16 = f32[4,24,128,128]{2,1,3,0:T(8,128)} copy(f32[4,24,128,128]{3,1,2,0:T(8,128)} %fusion.3) | data formatting | bytes 12582912 | tf_op jit(solution)/shard_map/ski,sbkl->sbil/dot_general | solution.py:30
  18.2 0.0 copy-done.2
  18.2 7.3 %broadcast_multiply_fusion = f32[4,24,128,128]{3,1,2,0:T(8,128)S(1)} fusion(f32[4]{0:T(128)S(1)} %and_convert_fusion, f32[4,24,128,128]{2,1,3,0:T(8,128)} %copy.16, f32[1,4,24,24]{3,2,1,0:T(8,128)S(1)} %copy-done.2, f32[24,24]{1,0:T(8,128)S(1)} %convert_element_type.20), kind=kOutput, calls=%fused_computation.5 | convolution fusion | flops 454560000 | bytes 12594448 | tf_op jit(solution)/shard_map/sbc,sbil->scil/dot_general | solution.py:31
  25.6 0.3 slice_bitcast_fusion.2
  25.9 2.6 %collective-permute-start = (f32[24,128,128]{2,0,1:T(8,128)S(1)}, f32[24,128,128]{2,0,1:T(8,128)S(1)}, u32[]{:S(2)}, u32[]{:S(2)}) collective-permute-start(f32[24,128,128]{2,0,1:T(8,128)S(1)} %get-tuple-element.6), channel_id=1, source_target_pairs={{0,1},{1,2},{2,3},{3,4},{4,5},{5,6},{6,7},{7,8},{8,9},{9,10},{10,1... | collective-permute-start | bytes 4718600 | tf_op jit(solution)/shard_map/ppermute | solution.py:13
  28.5 4.4 %collective-permute-start.2 = (f32[24,128,128]{2,0,1:T(8,128)S(1)}, f32[24,128,128]{2,0,1:T(8,128)S(1)}, u32[]{:S(2)}, u32[]{:S(2)}) collective-permute-start(f32[24,128,128]{2,0,1:T(8,128)S(1)} %get-tuple-element.7), channel_id=1, source_target_pairs={{0,9},{1,10},{2,11},{3,12},{4,13},{5,14},{6,15},{7,16},{8,17},{9,1... | collective-permute-start | bytes 4718600 | tf_op jit(solution)/shard_map/ppermute | solution.py:13
  32.9 3.4 %collective-permute-start.1 = (f32[24,128,128]{2,0,1:T(8,128)S(1)}, f32[24,128,128]{2,0,1:T(8,128)S(1)}, u32[]{:S(2)}, u32[]{:S(2)}) collective-permute-start(f32[24,128,128]{2,0,1:T(8,128)S(1)} %get-tuple-element.8), channel_id=1, source_target_pairs={{0,8},{1,9},{2,10},{3,11},{4,12},{5,13},{6,14},{7,15},{8,16},{9,17... | collective-permute-start | bytes 4718600 | tf_op jit(solution)/shard_map/ppermute | solution.py:13
  36.3 28.2 %collective-permute-done = f32[24,128,128]{2,0,1:T(8,128)S(1)} collective-permute-done((f32[24,128,128]{2,0,1:T(8,128)S(1)}, f32[24,128,128]{2,0,1:T(8,128)S(1)}, u32[]{:S(2)}, u32[]{:S(2)}) %collective-permute-start) | collective-permute-done | bytes 1572896 | tf_op jit(solution)/shard_map/ppermute | solution.py:13
  64.4 101.8 %collective-permute-done.2 = f32[24,128,128]{2,0,1:T(8,128)S(1)} collective-permute-done((f32[24,128,128]{2,0,1:T(8,128)S(1)}, f32[24,128,128]{2,0,1:T(8,128)S(1)}, u32[]{:S(2)}, u32[]{:S(2)}) %collective-permute-start.2) | collective-permute-done | bytes 1572896 | tf_op jit(solution)/shard_map/ppermute | solution.py:13
  166.3 67.5 %collective-permute-done.1 = f32[24,128,128]{2,0,1:T(8,128)S(1)} collective-permute-done((f32[24,128,128]{2,0,1:T(8,128)S(1)}, f32[24,128,128]{2,0,1:T(8,128)S(1)}, u32[]{:S(2)}, u32[]{:S(2)}) %collective-permute-start.1) | collective-permute-done | bytes 1572896 | tf_op jit(solution)/shard_map/ppermute | solution.py:13
  233.8 0.4 fusion.10
  234.2 1.9 collective-permute-start.3
  236.2 1.1 copy.11
  237.2 10.3 %collective-permute-done.3 = bf16[24,128,128]{2,0,1:T(8,128)(2,1)S(1)} collective-permute-done((bf16[24,128,128]{2,0,1:T(8,128)(2,1)S(1)}, bf16[24,128,128]{2,0,1:T(8,128)(2,1)S(1)}, u32[]{:S(2)}, u32[]{:S(2)}) %collective-permute-start.3) | collective-permute-done | bytes 786464 | tf_op jit(solution)/shard_map/ppermute | solution.py:13
  247.5 1.1 copy.12
  (2 shorter events, 0.0 us)
Async XLA Ops:
  0.6 3.7 %copy-start = (bf16[1,1,24,128,128]{4,3,2,1,0:T(8,128)(2,1)S(1)}, bf16[1,1,24,128,128]{4,3,2,1,0:T(8,128)(2,1)}, u32[]{:S(2)}) copy-start(bf16[1,1,24,128,128]{4,3,2,1,0:T(8,128)(2,1)} %param.6) | copy-start | bytes 2359300
  0.6 5.7 %copy-start.1 = (bf16[1,1,4,128,128]{4,3,2,1,0:T(8,128)(2,1)S(1)}, bf16[1,1,4,128,128]{4,3,2,1,0:T(8,128)(2,1)}, u32[]{:S(2)}) copy-start(bf16[1,1,4,128,128]{4,3,2,1,0:T(8,128)(2,1)} %param.5) | copy-start | bytes 393220
  11.7 6.5 %copy-start.2 = (f32[1,4,24,24]{3,2,1,0:T(8,128)S(1)}, f32[1,4,24,24]{3,2,1,0:T(8,128)}, u32[]{:S(2)}) copy-start(f32[1,4,24,24]{3,2,1,0:T(8,128)} %param.7) | copy-start | bytes 27652
  25.9 38.6 %collective-permute-start = (f32[24,128,128]{2,0,1:T(8,128)S(1)}, f32[24,128,128]{2,0,1:T(8,128)S(1)}, u32[]{:S(2)}, u32[]{:S(2)}) collective-permute-start(f32[24,128,128]{2,0,1:T(8,128)S(1)} %get-tuple-element.6), channel_id=1, source_target_pairs={{0,1},{1,2},{2,3},{3,4},{4,5},{5,6},{6,7},{7,8},{8,9},{9,10},{10,1... | collective-permute-start | bytes 4718600 | tf_op jit(solution)/shard_map/ppermute | solution.py:13
  28.5 137.8 %collective-permute-start.2 = (f32[24,128,128]{2,0,1:T(8,128)S(1)}, f32[24,128,128]{2,0,1:T(8,128)S(1)}, u32[]{:S(2)}, u32[]{:S(2)}) collective-permute-start(f32[24,128,128]{2,0,1:T(8,128)S(1)} %get-tuple-element.7), channel_id=1, source_target_pairs={{0,9},{1,10},{2,11},{3,12},{4,13},{5,14},{6,15},{7,16},{8,17},{9,1... | collective-permute-start | bytes 4718600 | tf_op jit(solution)/shard_map/ppermute | solution.py:13
  32.9 200.9 %collective-permute-start.1 = (f32[24,128,128]{2,0,1:T(8,128)S(1)}, f32[24,128,128]{2,0,1:T(8,128)S(1)}, u32[]{:S(2)}, u32[]{:S(2)}) collective-permute-start(f32[24,128,128]{2,0,1:T(8,128)S(1)} %get-tuple-element.8), channel_id=1, source_target_pairs={{0,8},{1,9},{2,10},{3,11},{4,12},{5,13},{6,14},{7,15},{8,16},{9,17... | collective-permute-start | bytes 4718600 | tf_op jit(solution)/shard_map/ppermute | solution.py:13
  234.2 13.3 %collective-permute-start.3 = (bf16[24,128,128]{2,0,1:T(8,128)(2,1)S(1)}, bf16[24,128,128]{2,0,1:T(8,128)(2,1)S(1)}, u32[]{:S(2)}, u32[]{:S(2)}) collective-permute-start(bf16[24,128,128]{2,0,1:T(8,128)(2,1)S(1)} %fusion.10), channel_id=1, source_target_pairs={{0,64},{64,128},{128,192},{192,256},{256,320},{320,384},{384,448},... | collective-permute-start | bytes 2359304 | tf_op jit(solution)/shard_map/ppermute | solution.py:13
where the time goes:
time: 249 us
  waiting for transfers between devices  208 us (84%)
  matrix products  14.6 us (6%)
  starting transfers between devices  12.3 us (5%)
  local copies, waits for them, and re-layouts  8.98 us (4%)
  other arithmetic  4.09 us (2%)
    ppermute x4, waiting for transfers between devices, passed_along(): return lax.ppermute(shard, axis, pairs)  208 us
    ppermute x4, starting transfers between devices, passed_along(): return lax.ppermute(shard, axis, pairs)  12.3 us
    dot_general x1, matrix products, finish(): jnp.einsum('sbc,sbil->scil', mixing, sandwich, precision=lax.Precision.HI...  7.33 us
    dot_general x1, local copies, waits for them, and re-layouts, finish(): jnp.einsum('ski,sbkl->sbil', blocks, halfway, preferred_element_type=jnp....  6.54 us
    dot_general x1, matrix products, finish(): jnp.einsum('ski,sbkl->sbil', blocks, halfway, preferred_element_type=jnp....  5.32 us
  transfers between devices with their start and end apart: 4, of which 4 were waited for; matrix products, arithmetic and copies ran while one was open for 0% of the time, Pallas kernels for 0%

commit v1 on v0

v1 whole, which is shorter than its diff:
```python
import functools

import jax
import jax.numpy as jnp
from jax import lax
from jax.experimental import pallas as pl
from jax.experimental.pallas import tpu as pltpu
from jax.sharding import PartitionSpec as P

STATES = 4
CHARGES = 8
BLOCK = 128
CHANNELS = 24
SECTORS = 64
TILE = 16
ROWS = CHANNELS * TILE
SPLITS = ((0, 12), (12, 24))

VMEM = pl.BlockSpec(memory_space=pltpu.VMEM)
SMEM = pl.BlockSpec(memory_space=pltpu.SMEM)


def passed_along(shard, axis, by):
    devices = lax.axis_size(axis)
    pairs = [(i, i + by) for i in range(devices) if 0 <= i + by < devices]
    if axis == "sec" and by == 1:
        pairs = [(i, j) for i, j in pairs if j % CHARGES]
    return lax.ppermute(shard, axis, pairs)


def two_terms(x):
    high = x.astype(jnp.bfloat16)
    low = (x - high.astype(jnp.float32)).astype(jnp.bfloat16)
    return high, low


def spread_weights(weights):
    row_channel = lax.broadcasted_iota(jnp.int32, (ROWS, CHANNELS), 0) // TILE
    channel = lax.broadcasted_iota(jnp.int32, (ROWS, CHANNELS), 1)
    onehot = (row_channel == channel).astype(jnp.bfloat16)
    row = lax.broadcasted_iota(jnp.int32, (ROWS, ROWS), 0) % TILE
    col = lax.broadcasted_iota(jnp.int32, (ROWS, ROWS), 1) % TILE
    same = row == col
    parts = []
    for term in two_terms(weights):
        by_row = lax.dot_general(onehot, term, (((1,), (1,)), ((), ())), preferred_element_type=jnp.float32)
        full = lax.dot_general(
            by_row.astype(jnp.bfloat16), onehot, (((1,), (1,)), ((), ())), preferred_element_type=jnp.float32
        )
        parts.append(jnp.where(same, full, 0.0).astype(jnp.bfloat16))
    return jnp.concatenate(parts, axis=1)


def masked(block, rows, cols):
    row = lax.broadcasted_iota(jnp.int32, (BLOCK, BLOCK), 0)
    col = lax.broadcasted_iota(jnp.int32, (BLOCK, BLOCK), 1)
    return jnp.where((row < rows) & (col < cols), block.astype(jnp.float32), 0.0)


def update(cur_ref, block, spread, count, mixed_ref, emit):
    for pair in range(BLOCK // (2 * TILE)):
        first = pair * 2 * TILE
        left = cur_ref[:, first : first + TILE, :].reshape(ROWS, BLOCK)
        right = cur_ref[:, first + TILE : first + 2 * TILE, :].reshape(ROWS, BLOCK)
        both = jnp.concatenate([left, right], axis=1)
        both = jnp.concatenate([both, both], axis=0)
        mixed = jnp.dot(spread, both, preferred_element_type=jnp.float32)
        for half in range(2):
            at = first + half * TILE
            part = mixed[:, half * BLOCK : (half + 1) * BLOCK].reshape(count, TILE, BLOCK)
            high, low = two_terms(part)
            mixed_ref[:count, at : at + TILE, :BLOCK] = high
            mixed_ref[:count, at : at + TILE, BLOCK:] = low
    stacked = block.astype(jnp.bfloat16)
    stacked = jnp.concatenate([stacked, stacked], axis=0)
    turned = block.T.astype(jnp.bfloat16)
    turned = jnp.concatenate([turned, turned], axis=1)
    for c in range(0, count, 2):
        rows = mixed_ref[c : c + 2].reshape(2 * BLOCK, 2 * BLOCK)
        half = jnp.dot(rows, stacked, preferred_element_type=jnp.float32)
        high, low = two_terms(half)
        first = jnp.concatenate([high[:BLOCK], high[BLOCK:]], axis=1)
        second = jnp.concatenate([low[:BLOCK], low[BLOCK:]], axis=1)
        pairs = jnp.concatenate([first, second], axis=0)
        result = jnp.dot(turned, pairs, preferred_element_type=jnp.float32)
        emit(c, result[:, :BLOCK], result[:, BLOCK:])


def sizes_of(sizes_ref, position):
    return sizes_ref[jnp.clip(position, 0, SECTORS - 1)]


def weights_of(couplings_ref, pattern_ref, state):
    return couplings_ref[state] * pattern_ref[...].astype(jnp.float32)


def own_kernel(sizes_ref, cur_ref, tensors_ref, couplings_ref, pattern_ref, keep_ref, pass_ref, spread_ref, mixed_ref):
    sector = lax.axis_index("sec")
    rows = sizes_of(sizes_ref, sector)
    for state, out in ((2, pass_ref), (0, keep_ref)):
        cols = sizes_of(sizes_ref, sector + state // 2 * CHARGES)
        block = masked(tensors_ref[state], rows, cols)
        spread = spread_weights(weights_of(couplings_ref, pattern_ref, state))

        def emit(c, first, second, out=out):
            out[c] = first
            out[c + 1] = second

        update(cur_ref, block, spread, CHANNELS, mixed_ref, emit)
    for at, state in enumerate((1, 3)):
        spread_ref[at] = spread_weights(weights_of(couplings_ref, pattern_ref, state))


def moved_kernel(state, low, high, sizes_ref, cur_ref, tensors_ref, spread_ref, base_ref, out_ref, mixed_ref):
    sector = lax.axis_index("sec")
    rows = sizes_of(sizes_ref, sector - 1)
    cols = sizes_of(sizes_ref, sector + state // 2 * CHARGES)
    block = masked(tensors_ref[state // 2], rows, cols)
    spread = spread_ref[state // 2, low * TILE : high * TILE, :]

    def emit(c, first, second):
        out_ref[c] = (base_ref[low + c] + first).astype(out_ref.dtype)
        out_ref[c + 1] = (base_ref[low + c + 1] + second).astype(out_ref.dtype)

    update(cur_ref, block, spread, high - low, mixed_ref, emit)


def scratch(count):
    return [pltpu.VMEM((count, BLOCK, 2 * BLOCK), jnp.bfloat16)]


PARAMS = pltpu.CompilerParams(vmem_limit_bytes=32 * 1024 * 1024)


def own(sizes, cur, tensors, couplings, pattern):
    full = jax.ShapeDtypeStruct((CHANNELS, BLOCK, BLOCK), jnp.float32)
    return pl.pallas_call(
        own_kernel,
        out_shape=(full, full, jax.ShapeDtypeStruct((2, ROWS, 2 * ROWS), jnp.bfloat16)),
        in_specs=[SMEM, VMEM, VMEM, VMEM, VMEM],
        out_specs=(VMEM, VMEM, VMEM),
        scratch_shapes=scratch(CHANNELS),
        compiler_params=PARAMS,
        name="own",
    )(sizes, cur, tensors, couplings, pattern)


def moved(state, low, high, dtype, sizes, cur, tensors, spread, base):
    return pl.pallas_call(
        functools.partial(moved_kernel, state, low, high),
        out_shape=jax.ShapeDtypeStruct((high - low, BLOCK, BLOCK), dtype),
        in_specs=[SMEM, VMEM, VMEM, VMEM, VMEM],
        out_specs=VMEM,
        scratch_shapes=scratch(high - low),
        compiler_params=PARAMS,
        name=f"moved_{state}_{low}",
    )(sizes, cur, tensors, spread, base)


def total_kernel(low, high, kept_ref, part_ref, out_ref):
    out_ref[...] = (kept_ref[low:high] + part_ref[...].astype(jnp.float32)).astype(jnp.bfloat16)


def total(low, high, kept, part):
    return pl.pallas_call(
        functools.partial(total_kernel, low, high),
        out_shape=jax.ShapeDtypeStruct(part.shape, jnp.bfloat16),
        in_specs=[VMEM, VMEM],
        out_specs=VMEM,
        compiler_params=PARAMS,
        name=f"total_{low}",
    )(kept, part)


def per_device(site_tensors, boundary, couplings, pattern, block_sizes):
    cur = boundary[0, 0]
    tensors = site_tensors[0, 0]
    cur_before = passed_along(cur, "sec", 1)
    tensors_before = passed_along(tensors[1::2], "sec", 1)
    kept, passing, spread = own(block_sizes, cur, tensors, couplings[0], pattern)
    arrived = []
    for low, high in SPLITS:
        sent = moved(3, low, high, jnp.bfloat16, block_sizes, cur_before, tensors_before, spread, passing)
        arrived.append(passed_along(sent, "sec", CHARGES))
    kept = moved(1, 0, CHANNELS, jnp.float32, block_sizes, cur_before, tensors_before, spread, kept)
    done, handed = [], []
    for (low, high), part in zip(SPLITS, arrived):
        result = total(low, high, kept, part)
        done.append(result)
        handed.append(passed_along(result, "seg", 1))
    return jnp.concatenate(done)[None, None], jnp.concatenate(handed)[None, None]


def solution(mesh):
    return jax.shard_map(
        per_device,
        mesh=mesh,
        in_specs=(
            P("seg", "sec", None, None, None),
            P("seg", "sec", None, None, None),
            P("seg", None, None, None),
            P(),
            P(),
        ),
        out_specs=(P("seg", "sec", None, None, None), P("seg", "sec", None, None, None)),
        check_vma=False,
    )
```

time: 249 us -> 75.8 us (0.30)
  the two profiles are of different devices: /device:TPU:316 before, /device:TPU:142 now
where the time goes in v1:
time: 75.8 us; the launch traced here: 75.3 us
  waiting for transfers between devices  27 us (36%)
  starting transfers between devices  22.1 us (29%)
  Pallas kernels  18.6 us (25%)
  local copies, waits for them, and re-layouts  5.04 us (7%)
  other arithmetic  1.9 us (3%)
    ppermute x6, waiting for transfers between devices, passed_along(): return lax.ppermute(shard, axis, pairs)  27 us
    ppermute x6, starting transfers between devices, passed_along(): return lax.ppermute(shard, axis, pairs)  22.1 us
    pallas_call x1, Pallas kernels, own(): pl.pallas_call(own_kernel, out_shape=(full, full, jax.ShapeDtypeStruct((2...  9.27 us
    pallas_call x3, Pallas kernels, moved(): pl.pallas_call(functools.partial(moved_kernel, state, low, high), out_sha...  9.17 us
    unnamed x10, local copies, waits for them, and re-layouts  4.19 us
  transfers between devices with their start and end apart: 6, of which 3 were waited for; matrix products, arithmetic and copies ran while one was open for 2% of the time, Pallas kernels for 21%

profile of v1, /device:TPU:142, one launch (start us, length us, event | category | flops | bytes accessed | tf_op | source)
XLA Modules:
  0.0 75.3 jit_solution(7070554073443280684)
XLA Ops:
  0.6 3.5 %collective-permute-start = (bf16[24,128,128]{2,1,0:T(8,128)(2,1)}, bf16[24,128,128]{2,1,0:T(8,128)(2,1)S(1)}, u32[]{:S(2)}, u32[]{:S(2)}) collective-permute-start(bf16[24,128,128]{2,1,0:T(8,128)(2,1)} %bitcast.7), channel_id=1, source_target_pairs={{0,1},{1,2},{2,3},{3,4},{4,5},{5,6},{6,7},{8,9},{9,10},{10,11},{11... | collective-permute-start | bytes 2359304 | tf_op jit(solution)/shard_map/ppermute | solution.py:28
  4.1 0.9 %slice.3 = bf16[2,128,128]{2,1,0:T(8,128)(2,1)S(1)} slice(bf16[4,128,128]{2,1,0:T(8,128)(2,1)} %bitcast.9), slice={[1:4:2], [0:128:1], [0:128:1]} | slice | bytes 131072 | tf_op jit(solution)/shard_map/slice | solution.py:179
  5.0 3.2 %collective-permute-start.1 = (bf16[2,128,128]{2,1,0:T(8,128)(2,1)S(1)}, bf16[2,128,128]{2,1,0:T(8,128)(2,1)S(1)}, u32[]{:S(2)}, u32[]{:S(2)}) collective-permute-start(bf16[2,128,128]{2,1,0:T(8,128)(2,1)S(1)} %slice.3), channel_id=1, source_target_pairs={{0,1},{1,2},{2,3},{3,4},{4,5},{5,6},{6,7},{8,9},{9,10},{10,11},{11... | collective-permute-start | bytes 196616 | tf_op jit(solution)/shard_map/ppermute | solution.py:28
  8.2 0.0 copy-start
  8.2 1.1 %copy-done = bf16[1,1,24,128,128]{4,3,2,1,0:T(8,128)(2,1)S(1)} copy-done((bf16[1,1,24,128,128]{4,3,2,1,0:T(8,128)(2,1)S(1)}, bf16[1,1,24,128,128]{4,3,2,1,0:T(8,128)(2,1)}, u32[]{:S(2)}) %copy-start) | copy-done | bytes 786456
  9.3 0.0 copy-start.1
  9.3 0.9 %copy-done.1 = bf16[1,1,4,128,128]{4,3,2,1,0:T(8,128)(2,1)S(1)} copy-done((bf16[1,1,4,128,128]{4,3,2,1,0:T(8,128)(2,1)S(1)}, bf16[1,1,4,128,128]{4,3,2,1,0:T(8,128)(2,1)}, u32[]{:S(2)}) %copy-start.1) | copy-done | bytes 131096
  10.2 0.0 copy-start.2
  10.2 0.8 %copy-done.2 = f32[1,4,24,24]{3,2,1,0:T(8,128)S(1)} copy-done((f32[1,4,24,24]{3,2,1,0:T(8,128)S(1)}, f32[1,4,24,24]{3,2,1,0:T(8,128)}, u32[]{:S(2)}) %copy-start.2) | copy-done | bytes 9240
  11.0 0.0 copy-start.3
  11.0 0.7 copy-done.3
  11.7 0.0 copy-start.4
  11.7 0.7 copy-done.4
  12.4 9.3 %own.1 = (f32[24,128,128]{2,1,0:T(8,128)S(1)}, f32[24,128,128]{2,1,0:T(8,128)S(1)}, bf16[2,384,768]{2,1,0:T(8,128)(2,1)S(1)}) custom-call(s32[64]{0:T(128)S(1)} %copy-done.4, bf16[24,128,128]{2,1,0:T(8,128)(2,1)S(1)} %bitcast.8, bf16[4,128,128]{2,1,0:T(8,128)(2,1)S(1)} %bitcast.10, f32[4,24,24]{2,1,0:T(8,128)S(1)} %bitcast.11, s32[24,24]{1,0:T(8,128)S(1)} %copy-done.3), custom_call_target="tpu_custom_call" | custom-call | tf_op jit(solution)/shard_map/own/pallas_call | solution.py:137
  21.6 1.8 %collective-permute-done.1.tensors_ref = bf16[2,128,128]{2,1,0:T(8,128)(2,1)S(1)} collective-permute-done((bf16[2,128,128]{2,1,0:T(8,128)(2,1)S(1)}, bf16[2,128,128]{2,1,0:T(8,128)(2,1)S(1)}, u32[]{:S(2)}, u32[]{:S(2)}) %collective-permute-start.1) | collective-permute-done | bytes 65568 | tf_op jit(solution)/shard_map/ppermute | solution.py:28
  23.4 0.0 collective-permute-done.cur_ref
  23.4 2.5 %moved_3_0.1 = bf16[12,128,128]{2,1,0:T(8,128)(2,1)S(1)} custom-call(s32[64]{0:T(128)S(1)} %copy-done.4, bf16[24,128,128]{2,1,0:T(8,128)(2,1)S(1)} %collective-permute-done.cur_ref, bf16[2,128,128]{2,1,0:T(8,128)(2,1)S(1)} %collective-permute-done.1.tensors_ref, bf16[2,384,768]{2,1,0:T(8,128)(2,1)S(1)} %get-tuple-element.5.spread_ref, ...), custom_call_target="tpu_custom_call" | custom-call | tf_op jit(solution)/shard_map/moved_3_0/pallas_call | solution.py:149
  25.9 5.2 %collective-permute-start.2 = (bf16[12,128,128]{2,1,0:T(8,128)(2,1)S(1)}, bf16[12,128,128]{2,1,0:T(8,128)(2,1)S(1)}, u32[]{:S(2)}, u32[]{:S(2)}) collective-permute-start(bf16[12,128,128]{2,1,0:T(8,128)(2,1)S(1)} %moved_3_0.1), channel_id=1, source_target_pairs={{0,8},{1,9},{2,10},{3,11},{4,12},{5,13},{6,14},{7,15},{8,16},{9,17... | collective-permute-start | bytes 1179656 | tf_op jit(solution)/shard_map/ppermute | solution.py:28
  31.1 2.5 %moved_3_12.1 = bf16[12,128,128]{2,1,0:T(8,128)(2,1)S(1)} custom-call(s32[64]{0:T(128)S(1)} %copy-done.4, bf16[24,128,128]{2,1,0:T(8,128)(2,1)S(1)} %collective-permute-done.cur_ref, bf16[2,128,128]{2,1,0:T(8,128)(2,1)S(1)} %collective-permute-done.1.tensors_ref, bf16[2,384,768]{2,1,0:T(8,128)(2,1)S(1)} %get-tuple-element.5.spread_ref, ...), custom_call_target="tpu_custom_call" | custom-call | tf_op jit(solution)/shard_map/moved_3_12/pallas_call | solution.py:149
  33.6 6.4 %collective-permute-start.3 = (bf16[12,128,128]{2,1,0:T(8,128)(2,1)S(1)}, bf16[12,128,128]{2,1,0:T(8,128)(2,1)S(1)}, u32[]{:S(2)}, u32[]{:S(2)}) collective-permute-start(bf16[12,128,128]{2,1,0:T(8,128)(2,1)S(1)} %moved_3_12.1), channel_id=1, source_target_pairs={{0,8},{1,9},{2,10},{3,11},{4,12},{5,13},{6,14},{7,15},{8,16},{9,17... | collective-permute-start | bytes 1179656 | tf_op jit(solution)/shard_map/ppermute | solution.py:28
  40.0 4.2 %moved_1_0.1.kept_ref = f32[24,128,128]{2,1,0:T(8,128)S(1)} custom-call(s32[64]{0:T(128)S(1)} %copy-done.4, bf16[24,128,128]{2,1,0:T(8,128)(2,1)S(1)} %collective-permute-done.cur_ref, bf16[2,128,128]{2,1,0:T(8,128)(2,1)S(1)} %collective-permute-done.1.tensors_ref, bf16[2,384,768]{2,1,0:T(8,128)(2,1)S(1)} %get-tuple-element.5.spread_ref, ...), custom_call_target="tpu_custom_call" | custom-call | tf_op jit(solution)/shard_map/moved_1_0/pallas_call | solution.py:149
  44.2 0.0 collective-permute-done.2.part_ref
  44.2 0.1 total_0.1
  44.3 1.9 %collective-permute-start.4 = (bf16[12,128,128]{2,1,0:T(8,128)(2,1)S(1)}, bf16[12,128,128]{2,1,0:T(8,128)(2,1)S(1)}, u32[]{:S(2)}, u32[]{:S(2)}) collective-permute-start(bf16[12,128,128]{2,1,0:T(8,128)(2,1)S(1)} %total_0.1), channel_id=1, source_target_pairs={{0,64},{64,128},{128,192},{192,256},{256,320},{320,384},{384,448},... | collective-permute-start | bytes 1179656 | tf_op jit(solution)/shard_map/ppermute | solution.py:28
  46.2 19.0 %collective-permute-done.3.part_ref = bf16[12,128,128]{2,1,0:T(8,128)(2,1)S(1)} collective-permute-done((bf16[12,128,128]{2,1,0:T(8,128)(2,1)S(1)}, bf16[12,128,128]{2,1,0:T(8,128)(2,1)S(1)}, u32[]{:S(2)}, u32[]{:S(2)}) %collective-permute-start.3) | collective-permute-done | bytes 393248 | tf_op jit(solution)/shard_map/ppermute | solution.py:28
  65.2 0.1 total_12.1
  65.3 1.9 %collective-permute-start.5 = (bf16[12,128,128]{2,1,0:T(8,128)(2,1)S(1)}, bf16[12,128,128]{2,1,0:T(8,128)(2,1)S(1)}, u32[]{:S(2)}, u32[]{:S(2)}) collective-permute-start(bf16[12,128,128]{2,1,0:T(8,128)(2,1)S(1)} %total_12.1), channel_id=1, source_target_pairs={{0,64},{64,128},{128,192},{192,256},{256,320},{320,384},{384,448},... | collective-permute-start | bytes 1179656 | tf_op jit(solution)/shard_map/ppermute | solution.py:28
  67.2 0.9 %maximum_bitcast_fusion = bf16[1,1,24,128,128]{4,3,2,1,0:T(8,128)(2,1)} fusion(bf16[12,128,128]{2,1,0:T(8,128)(2,1)S(1)} %total_12.1, bf16[12,128,128]{2,1,0:T(8,128)(2,1)S(1)} %total_0.1), kind=kLoop, calls=%fused_computation | loop fusion | flops 393216 | bytes 1572864 | tf_op jit(solution)/shard_map/broadcast_in_dim | solution.py:191
  68.2 0.0 collective-permute-done.4
  68.2 6.2 %collective-permute-done.5 = bf16[12,128,128]{2,1,0:T(8,128)(2,1)S(1)} collective-permute-done((bf16[12,128,128]{2,1,0:T(8,128)(2,1)S(1)}, bf16[12,128,128]{2,1,0:T(8,128)(2,1)S(1)}, u32[]{:S(2)}, u32[]{:S(2)}) %collective-permute-start.5) | collective-permute-done | bytes 393248 | tf_op jit(solution)/shard_map/ppermute | solution.py:28
  74.4 0.9 %maximum_bitcast_fusion.1 = bf16[1,1,24,128,128]{4,3,2,1,0:T(8,128)(2,1)} fusion(bf16[12,128,128]{2,1,0:T(8,128)(2,1)S(1)} %collective-permute-done.5, bf16[12,128,128]{2,1,0:T(8,128)(2,1)S(1)} %collective-permute-done.4), kind=kLoop, calls=%fused_computation.1 | loop fusion | flops 393216 | bytes 1572864 | tf_op jit(solution)/shard_map/broadcast_in_dim | solution.py:191
Async XLA Ops:
  0.6 22.8 %collective-permute-start = (bf16[24,128,128]{2,1,0:T(8,128)(2,1)}, bf16[24,128,128]{2,1,0:T(8,128)(2,1)S(1)}, u32[]{:S(2)}, u32[]{:S(2)}) collective-permute-start(bf16[24,128,128]{2,1,0:T(8,128)(2,1)} %bitcast.7), channel_id=1, source_target_pairs={{0,1},{1,2},{2,3},{3,4},{4,5},{5,6},{6,7},{8,9},{9,10},{10,11},{11... | collective-permute-start | bytes 2359304 | tf_op jit(solution)/shard_map/ppermute | solution.py:28
  5.0 18.4 %collective-permute-start.1 = (bf16[2,128,128]{2,1,0:T(8,128)(2,1)S(1)}, bf16[2,128,128]{2,1,0:T(8,128)(2,1)S(1)}, u32[]{:S(2)}, u32[]{:S(2)}) collective-permute-start(bf16[2,128,128]{2,1,0:T(8,128)(2,1)S(1)} %slice.3), channel_id=1, source_target_pairs={{0,1},{1,2},{2,3},{3,4},{4,5},{5,6},{6,7},{8,9},{9,10},{10,11},{11... | collective-permute-start | bytes 196616 | tf_op jit(solution)/shard_map/ppermute | solution.py:28
  8.2 1.1 %copy-start = (bf16[1,1,24,128,128]{4,3,2,1,0:T(8,128)(2,1)S(1)}, bf16[1,1,24,128,128]{4,3,2,1,0:T(8,128)(2,1)}, u32[]{:S(2)}) copy-start(bf16[1,1,24,128,128]{4,3,2,1,0:T(8,128)(2,1)} %param.6) | copy-start | bytes 2359300
  9.3 0.9 %copy-start.1 = (bf16[1,1,4,128,128]{4,3,2,1,0:T(8,128)(2,1)S(1)}, bf16[1,1,4,128,128]{4,3,2,1,0:T(8,128)(2,1)}, u32[]{:S(2)}) copy-start(bf16[1,1,4,128,128]{4,3,2,1,0:T(8,128)(2,1)} %param.5) | copy-start | bytes 393220
  10.2 0.8 %copy-start.2 = (f32[1,4,24,24]{3,2,1,0:T(8,128)S(1)}, f32[1,4,24,24]{3,2,1,0:T(8,128)}, u32[]{:S(2)}) copy-start(f32[1,4,24,24]{3,2,1,0:T(8,128)} %param.7) | copy-start | bytes 27652
  11.0 0.7 copy-start.3
  11.7 0.7 copy-start.4
  25.9 18.3 %collective-permute-start.2 = (bf16[12,128,128]{2,1,0:T(8,128)(2,1)S(1)}, bf16[12,128,128]{2,1,0:T(8,128)(2,1)S(1)}, u32[]{:S(2)}, u32[]{:S(2)}) collective-permute-start(bf16[12,128,128]{2,1,0:T(8,128)(2,1)S(1)} %moved_3_0.1), channel_id=1, source_target_pairs={{0,8},{1,9},{2,10},{3,11},{4,12},{5,13},{6,14},{7,15},{8,16},{9,17... | collective-permute-start | bytes 1179656 | tf_op jit(solution)/shard_map/ppermute | solution.py:28
  33.6 31.6 %collective-permute-start.3 = (bf16[12,128,128]{2,1,0:T(8,128)(2,1)S(1)}, bf16[12,128,128]{2,1,0:T(8,128)(2,1)S(1)}, u32[]{:S(2)}, u32[]{:S(2)}) collective-permute-start(bf16[12,128,128]{2,1,0:T(8,128)(2,1)S(1)} %moved_3_12.1), channel_id=1, source_target_pairs={{0,8},{1,9},{2,10},{3,11},{4,12},{5,13},{6,14},{7,15},{8,16},{9,17... | collective-permute-start | bytes 1179656 | tf_op jit(solution)/shard_map/ppermute | solution.py:28
  44.3 23.9 %collective-permute-start.4 = (bf16[12,128,128]{2,1,0:T(8,128)(2,1)S(1)}, bf16[12,128,128]{2,1,0:T(8,128)(2,1)S(1)}, u32[]{:S(2)}, u32[]{:S(2)}) collective-permute-start(bf16[12,128,128]{2,1,0:T(8,128)(2,1)S(1)} %total_0.1), channel_id=1, source_target_pairs={{0,64},{64,128},{128,192},{192,256},{256,320},{320,384},{384,448},... | collective-permute-start | bytes 1179656 | tf_op jit(solution)/shard_map/ppermute | solution.py:28
  65.3 9.1 %collective-permute-start.5 = (bf16[12,128,128]{2,1,0:T(8,128)(2,1)S(1)}, bf16[12,128,128]{2,1,0:T(8,128)(2,1)S(1)}, u32[]{:S(2)}, u32[]{:S(2)}) collective-permute-start(bf16[12,128,128]{2,1,0:T(8,128)(2,1)S(1)} %total_12.1), channel_id=1, source_target_pairs={{0,64},{64,128},{128,192},{192,256},{256,320},{320,384},{384,448},... | collective-permute-start | bytes 1179656 | tf_op jit(solution)/shard_map/ppermute | solution.py:28

commit v2 on v0

v2 whole, which is shorter than its diff:
```python
import functools

import jax
import jax.numpy as jnp
from jax import lax
from jax.experimental import pallas as pl
from jax.experimental.pallas import tpu as pltpu
from jax.sharding import PartitionSpec as P

STATES = 4
CHARGES = 8
BLOCK = 128
CHANNELS = 24
SECTORS = 64
TILE = 16
ROWS = CHANNELS * TILE
CUTS = (0, 6, 12, 18, 24)
CHUNKS = tuple(zip(CUTS[:-1], CUTS[1:]))
VMEM = pl.BlockSpec(memory_space=pltpu.VMEM)
SMEM = pl.BlockSpec(memory_space=pltpu.SMEM)
HBM = pl.BlockSpec(memory_space=pltpu.HBM)
ANY = pl.BlockSpec(memory_space=pl.ANY)
PARAMS = pltpu.CompilerParams(vmem_limit_bytes=32 * 1024 * 1024)
MIXED = pltpu.VMEM((CHANNELS, BLOCK, BLOCK), jnp.bfloat16)


def array(dtype, *shape):
    return jax.ShapeDtypeStruct(shape, dtype)


def send(shard, axis, by):
    devices = lax.axis_size(axis)
    pairs = [(i, i + by) for i in range(devices) if 0 <= i + by < devices]
    if axis == "sec" and by == 1:
        pairs = [(i, j) for i, j in pairs if j % CHARGES]
    return lax.ppermute(shard, axis, pairs)


def two_terms(x):
    high = x.astype(jnp.bfloat16)
    low = (x - high.astype(jnp.float32)).astype(jnp.bfloat16)
    return high, low


def spread_weights(weights, low, high):
    rows = (high - low) * TILE
    channel_of_row = lax.broadcasted_iota(jnp.int32, (rows, CHANNELS), 0) // TILE + low
    pick_c = (channel_of_row == lax.broadcasted_iota(jnp.int32, (rows, CHANNELS), 1)).astype(jnp.bfloat16)
    channel_of_row = lax.broadcasted_iota(jnp.int32, (ROWS, CHANNELS), 0) // TILE
    pick_b = (channel_of_row == lax.broadcasted_iota(jnp.int32, (ROWS, CHANNELS), 1)).astype(jnp.bfloat16)
    row = lax.broadcasted_iota(jnp.int32, (rows, ROWS), 0) % TILE
    col = lax.broadcasted_iota(jnp.int32, (rows, ROWS), 1) % TILE
    same = row == col
    contract = (((1,), (1,)), ((), ()))
    parts = []
    for term in two_terms(weights):
        by_row = lax.dot_general(pick_c, term, contract, preferred_element_type=jnp.float32)
        full = lax.dot_general(by_row.astype(jnp.bfloat16), pick_b, contract, preferred_element_type=jnp.float32)
        parts.append(jnp.where(same, full, 0.0).astype(jnp.bfloat16))
    return jnp.concatenate(parts, axis=1)


def update(cur_ref, block, spread, count, mixed_ref, emit):
    for first in range(0, BLOCK, 2 * TILE):
        left = cur_ref[:CHANNELS, first : first + TILE, :].reshape(ROWS, BLOCK)
        right = cur_ref[:CHANNELS, first + TILE : first + 2 * TILE, :].reshape(ROWS, BLOCK)
        both = jnp.concatenate([left, right], axis=1)
        both = jnp.concatenate([both, both], axis=0)
        mixed = jnp.dot(spread, both, preferred_element_type=jnp.float32).astype(jnp.bfloat16)
        for half in range(2):
            at = first + half * TILE
            mixed_ref[:count, at : at + TILE, :] = mixed[:, half * BLOCK : (half + 1) * BLOCK].reshape(count, TILE, BLOCK)
    left_block = block.astype(jnp.float32).T.astype(jnp.bfloat16)
    left_block = jnp.concatenate([left_block, left_block], axis=1)
    for c in range(0, count, 2):
        rows = mixed_ref[c : c + 2].reshape(2 * BLOCK, BLOCK)
        high, low = two_terms(jnp.dot(rows, block, preferred_element_type=jnp.float32))
        first = jnp.concatenate([high[:BLOCK], high[BLOCK:]], axis=1)
        second = jnp.concatenate([low[:BLOCK], low[BLOCK:]], axis=1)
        pairs = jnp.concatenate([first, second], axis=0)
        result = jnp.dot(left_block, pairs, preferred_element_type=jnp.float32)
        emit(c, result[:, :BLOCK])
        emit(c + 1, result[:, BLOCK:])


def masked(block, rows, cols):
    row = lax.broadcasted_iota(jnp.int32, (BLOCK, BLOCK), 0)
    col = lax.broadcasted_iota(jnp.int32, (BLOCK, BLOCK), 1)
    return jnp.where((row < rows) & (col < cols), block.astype(jnp.float32), 0.0).astype(jnp.bfloat16)


def loaded_kernel(sizes_hbm, cur_hbm, tensors_hbm, couplings_hbm, pattern_hbm, *refs):
    cur_ref, even_ref, odd_ref, weights_ref, sizes_ref, tensors_ref, pattern_ref, sems = refs
    copies = [
        pltpu.make_async_copy(source, target, sems.at[at])
        for at, (source, target) in enumerate(
            (
                (sizes_hbm, sizes_ref),
                (tensors_hbm, tensors_ref),
                (couplings_hbm, weights_ref),
                (pattern_hbm, pattern_ref),
                (cur_hbm, cur_ref),
            )
        )
    ]
    for copy in copies:
        copy.start()
    copies[0].wait()
    copies[1].wait()
    sector = lax.axis_index("sec")
    for state in range(STATES):
        target = jnp.minimum(sector + state // 2 * CHARGES + state % 2, SECTORS - 1)
        kept_ref = odd_ref if state % 2 else even_ref
        kept_ref[state // 2] = masked(tensors_ref[state], sizes_ref[sector], sizes_ref[target])
    copies[2].wait()
    copies[3].wait()
    pattern = pattern_ref[...].astype(jnp.float32)
    for state in range(STATES):
        weights_ref[state] = weights_ref[state] * pattern
    copies[4].wait()


COSTS = dict(
    loaded=1, own_2=1, own_0=1, kept=1,
    **{f"{kind}_{low}": 1 if kind == "sent" or low == CUTS[-2] else 10 for kind in ("sent", "total", "placed") for low in CUTS},
)


def cost(name):
    return pl.CostEstimate(flops=int(COSTS[name] * 2.5e9), bytes_accessed=1 << 20, transcendentals=0)


def loaded(sizes, cur, tensors, couplings, pattern):
    stay = [pltpu.with_memory_space_constraint(x, pltpu.HBM) for x in (sizes, cur, tensors, couplings, pattern)]
    return pl.pallas_call(
        loaded_kernel,
        out_shape=(
            array(jnp.bfloat16, CHANNELS, BLOCK, BLOCK),
            array(jnp.bfloat16, 2, BLOCK, BLOCK),
            array(jnp.bfloat16, 2, BLOCK, BLOCK),
            array(jnp.float32, STATES, CHANNELS, CHANNELS),
        ),
        in_specs=[HBM] * 5,
        out_specs=(VMEM,) * 4,
        scratch_shapes=[
            pltpu.SMEM((SECTORS,), jnp.int32),
            pltpu.VMEM((STATES, BLOCK, BLOCK), jnp.bfloat16),
            pltpu.VMEM((CHANNELS, CHANNELS), jnp.int32),
            pltpu.SemaphoreType.DMA((5,)),
        ],
        compiler_params=PARAMS,
        cost_estimate=cost("loaded"),
        name="loaded",
    )(*stay)


def own_kernel(state, cur_ref, even_ref, weights_ref, _, out_ref, spread_ref, mixed_ref):
    def emit(c, value):
        out_ref[c] = value

    spread = spread_weights(weights_ref[state], 0, CHANNELS)
    update(cur_ref, even_ref[state // 2], spread, CHANNELS, mixed_ref, emit)
    spread_ref[...] = spread_weights(weights_ref[state + 1], 0, CHANNELS)


def own(state, cur, even, weights, after):
    name = f"own_{state}"
    return pl.pallas_call(
        functools.partial(own_kernel, state),
        out_shape=(array(jnp.float32, CHANNELS, BLOCK, BLOCK), array(jnp.bfloat16, ROWS, 2 * ROWS)),
        in_specs=[VMEM] * 3 + [ANY],
        out_specs=(VMEM,) * 2,
        scratch_shapes=[MIXED],
        compiler_params=PARAMS,
        cost_estimate=cost(name),
        name=name,
    )(cur, even, weights, after)


def joined_kernel(state, low, high, base_ref, spread_ref, raw_ref, odd_ref, _, out_ref, mixed_ref):
    def emit(c, value):
        out_ref[c] = (base_ref[low + c] + value).astype(out_ref.dtype)

    spread = spread_ref[low * TILE : high * TILE, :]
    update(raw_ref, odd_ref[state // 2], spread, high - low, mixed_ref, emit)


def joined(name, state, low, high, dtype, base, spread, raw, odd, after):
    return pl.pallas_call(
        functools.partial(joined_kernel, state, low, high),
        out_shape=array(dtype, high - low, BLOCK, BLOCK),
        in_specs=[VMEM] * 4 + [ANY],
        out_specs=VMEM,
        scratch_shapes=[MIXED],
        compiler_params=PARAMS,
        cost_estimate=cost(name),
        name=name,
    )(base, spread, raw, odd, after)


def total_kernel(low, high, base_ref, up_ref, _, out_ref):
    out_ref[...] = (
        base_ref[low:high] + up_ref[...].astype(jnp.float32)
    ).astype(jnp.bfloat16)


def whole_of(part):
    return array(part.dtype, CHANNELS, BLOCK, BLOCK)


def total(low, high, base, up, after):
    return pl.pallas_call(
        functools.partial(total_kernel, low, high),
        out_shape=array(jnp.bfloat16, high - low, BLOCK, BLOCK),
        in_specs=[VMEM, VMEM, ANY],
        out_specs=VMEM,
        compiler_params=PARAMS,
        cost_estimate=cost(f"total_{low}"),
        name=f"total_{low}",
    )(base, up, after)


def placed_kernel(low, high, part_ref, *refs):
    whole_hbm, sem = refs[-2:]
    copy = pltpu.make_async_copy(part_ref, whole_hbm.at[low:high], sem)
    copy.start()
    copy.wait()


def placed(low, high, part, whole):
    given = [] if whole is None else [whole]
    return pl.pallas_call(
        functools.partial(placed_kernel, low, high),
        out_shape=whole_of(part),
        in_specs=[VMEM] + [HBM] * len(given),
        out_specs=HBM,
        scratch_shapes=[pltpu.SemaphoreType.DMA],
        input_output_aliases={1: 0} if given else {},
        compiler_params=PARAMS,
        cost_estimate=cost(f"placed_{low}"),
        name=f"placed_{low}",
    )(part, *given)


def per_device(site_tensors, boundary, couplings, pattern, sizes):
    raw = send(boundary[0, 0], "sec", 1)
    cur, even, odd, weights = loaded(sizes, boundary[0, 0], site_tensors[0, 0], couplings[0], pattern)
    odd = send(odd, "sec", 1)
    up, spread_up = own(2, cur, even, weights, weights)
    kept, spread_kept = own(0, cur, even, weights, up)
    arrived, done, handed = [], [], None
    last = kept

    def go_up(last):
        low, high = CHUNKS[len(arrived)]
        last = joined(f"sent_{low}", 3, low, high, jnp.bfloat16, up, spread_up, raw, odd, last)
        arrived.append(send(last, "sec", CHARGES))
        return last

    for _ in range(3):
        last = go_up(last)
    kept = last = joined("kept", 1, 0, CHANNELS, jnp.float32, kept, spread_kept, raw, odd, last)
    for at, (low, high) in enumerate(CHUNKS):
        last = total(low, high, kept, arrived[at], last)
        done.append(last)
        handed = placed(low, high, send(last, "seg", 1), handed)
        if len(arrived) < len(CHUNKS):
            last = go_up(last)
    return jnp.concatenate(done)[None, None], handed[None, None]


def solution(mesh):
    return jax.shard_map(
        per_device,
        mesh=mesh,
        in_specs=(
            P("seg", "sec", None, None, None),
            P("seg", "sec", None, None, None),
            P("seg", None, None, None),
            P(),
            P(),
        ),
        out_specs=(P("seg", "sec", None, None, None), P("seg", "sec", None, None, None)),
        check_vma=False,
    )
```

time: 249 us -> 72.2 us (0.29)
  waiting for transfers between devices: 208 us -> 33.7 us
  matrix products: 14.6 us -> 0 us
  Pallas kernels: 0 us -> 12.5 us
  starting transfers between devices: 12.3 us -> 23.7 us
  local copies, waits for them, and re-layouts: 8.98 us -> 0 us
  other arithmetic: 4.09 us -> 0.98 us
    ppermute x4 -> x10, waiting for transfers between devices: 208 us -> 33.7 us  [send(): return lax.ppermute(shard, axis, pairs)]
    dot_general x3 -> x0, matrix products: 14.6 us -> none  [the longest x1 7.33 us: finish(): jnp.einsum('sbc,sbil->scil', mixing, sandwich, precision=lax.Precision.HI...]
    pallas_call x0 -> x16, Pallas kernels: none -> 12.5 us  [the longest x5 4.31 us: joined(): pl.pallas_call(functools.partial(joined_kernel, state, low, high), out_sh...]
    ppermute x4 -> x10, starting transfers between devices: 12.3 us -> 23.7 us  [send(): return lax.ppermute(shard, axis, pairs)]
    dot_general x1 -> x0, local copies, waits for them, and re-layouts: 6.54 us -> none  [finish(): jnp.einsum('ski,sbkl->sbil', blocks, halfway, preferred_element_type=jnp....]
  transfers between devices with their start and end apart: 4 -> 10, of which waited for: 4 -> 4; matrix products, arithmetic and copies ran while one was open for 0% -> 1% of each run, Pallas kernels for 0% -> 15%
where the time goes in v2:
time: 72.2 us; the launch traced here: 71.8 us
  waiting for transfers between devices  33.7 us (47%)
  starting transfers between devices  23.7 us (33%)
  Pallas kernels  12.5 us (17%)
  other arithmetic  0.98 us (1%)
  between operations  0.86 us (1%)
    ppermute x10, waiting for transfers between devices, send(): return lax.ppermute(shard, axis, pairs)  33.7 us
    ppermute x10, starting transfers between devices, send(): return lax.ppermute(shard, axis, pairs)  23.7 us
    pallas_call x5, Pallas kernels, joined(): pl.pallas_call(functools.partial(joined_kernel, state, low, high), out_sh...  4.31 us
    pallas_call x2, Pallas kernels, own(): pl.pallas_call(functools.partial(own_kernel, state), out_shape=(array(jnp...  4.01 us
    pallas_call x4, Pallas kernels, placed(): pl.pallas_call(functools.partial(placed_kernel, low, high), out_shape=who...  2.75 us
  transfers between devices with their start and end apart: 10, of which 4 were waited for; matrix products, arithmetic and copies ran while one was open for 1% of the time, Pallas kernels for 15%

profile of v2, /device:TPU:316, one launch (start us, length us, event | category | flops | bytes accessed | tf_op | source)
XLA Modules:
  0.0 71.8 jit_solution(17459216074552996142)
XLA Ops:
  0.6 1.3 %collective-permute-start = (bf16[24,128,128]{2,1,0:T(8,128)(2,1)}, bf16[24,128,128]{2,1,0:T(8,128)(2,1)S(1)}, u32[]{:S(2)}, u32[]{:S(2)}) collective-permute-start(bf16[24,128,128]{2,1,0:T(8,128)(2,1)} %bitcast.6), channel_id=1, source_target_pairs={{0,1},{1,2},{2,3},{3,4},{4,5},{5,6},{6,7},{8,9},{9,10},{10,11},{11... | collective-permute-start | bytes 2359304 | tf_op jit(solution)/shard_map/ppermute | solution.py:36
  1.9 1.3 %loaded.1 = (bf16[24,128,128]{2,1,0:T(8,128)(2,1)S(1)}, bf16[2,128,128]{2,1,0:T(8,128)(2,1)S(1)}, bf16[2,128,128]{2,1,0:T(8,128)(2,1)S(1)}, f32[4,24,24]{2,1,0:T(8,128)S(1)}) custom-call(s32[64]{0:T(128)} %sizes_hbm.1, bf16[24,128,128]{2,1,0:T(8,128)(2,1)} %bitcast.7, bf16[4,128,128]{2,1,0:T(8,128)(2,1)} %bitcast.8, f32[4,24,24]{2,1,0:T(8,128)} %bitcast.9, ...), custom_call_target="tpu_custom_call" | custom-call | flops 2500000000 | bytes 1048576 | tf_op jit(solution)/shard_map/loaded/pallas_call | solution.py:135
  3.2 1.3 %collective-permute-start.1 = (bf16[2,128,128]{2,1,0:T(8,128)(2,1)S(1)}, bf16[2,128,128]{2,1,0:T(8,128)(2,1)S(1)}, u32[]{:S(2)}, u32[]{:S(2)}) collective-permute-start(bf16[2,128,128]{2,1,0:T(8,128)(2,1)S(1)} %get-tuple-element.16), channel_id=1, source_target_pairs={{0,1},{1,2},{2,3},{3,4},{4,5},{5,6},{6,7},{8,9},{9,10},{10,11},{11... | collective-permute-start | bytes 196616 | tf_op jit(solution)/shard_map/ppermute | solution.py:36
  4.5 2.0 %own_2.1 = (f32[24,128,128]{2,1,0:T(8,128)S(1)}, bf16[384,768]{1,0:T(8,128)(2,1)S(1)}) custom-call(bf16[24,128,128]{2,1,0:T(8,128)(2,1)S(1)} %get-tuple-element.10.cur_ref, bf16[2,128,128]{2,1,0:T(8,128)(2,1)S(1)} %get-tuple-element.11.even_ref, f32[4,24,24]{2,1,0:T(8,128)S(1)} %get-tuple-element.12.weights_ref._, ...), custom_call_target="tpu_custom_call" | custom-call | flops 2500000000 | bytes 1048576 | tf_op jit(solution)/shard_map/own_2/pallas_call | solution.py:168
  6.6 2.0 %own_0.1 = (f32[24,128,128]{2,1,0:T(8,128)S(1)}, bf16[384,768]{1,0:T(8,128)(2,1)S(1)}) custom-call(bf16[24,128,128]{2,1,0:T(8,128)(2,1)S(1)} %get-tuple-element.10.cur_ref, bf16[2,128,128]{2,1,0:T(8,128)(2,1)S(1)} %get-tuple-element.11.even_ref, f32[4,24,24]{2,1,0:T(8,128)S(1)} %get-tuple-element.12.weights_ref._, ...), custom_call_target="tpu_custom_call" | custom-call | flops 2500000000 | bytes 1048576 | tf_op jit(solution)/shard_map/own_0/pallas_call | solution.py:168
  8.6 14.9 %collective-permute-done.1.odd_ref = bf16[2,128,128]{2,1,0:T(8,128)(2,1)S(1)} collective-permute-done((bf16[2,128,128]{2,1,0:T(8,128)(2,1)S(1)}, bf16[2,128,128]{2,1,0:T(8,128)(2,1)S(1)}, u32[]{:S(2)}, u32[]{:S(2)}) %collective-permute-start.1) | collective-permute-done | bytes 65568 | tf_op jit(solution)/shard_map/ppermute | solution.py:36
  23.4 0.0 collective-permute-done.raw_ref
  23.4 0.7 %sent_0.1._ = bf16[6,128,128]{2,1,0:T(8,128)(2,1)S(1)} custom-call(f32[24,128,128]{2,1,0:T(8,128)S(1)} %get-tuple-element.13._.base_ref, bf16[384,768]{1,0:T(8,128)(2,1)S(1)} %get-tuple-element.17.spread_ref, bf16[24,128,128]{2,1,0:T(8,128)(2,1)S(1)} %collective-permute-done.raw_ref, bf16[2,128,128]{2,1,0:T(8,128)(2,1)S(1)} %collective-permute-done.1.odd_ref, ...), custom_call_target="tpu_custom_call" | custom-call | flops 2500000000 | bytes 1048576 | tf_op jit(solution)/shard_map/sent_0/pallas_call | solution.py:189
  24.2 3.4 %collective-permute-start.2 = (bf16[6,128,128]{2,1,0:T(8,128)(2,1)S(1)}, bf16[6,128,128]{2,1,0:T(8,128)(2,1)S(1)}, u32[]{:S(2)}, u32[]{:S(2)}) collective-permute-start(bf16[6,128,128]{2,1,0:T(8,128)(2,1)S(1)} %sent_0.1._), channel_id=1, source_target_pairs={{0,8},{1,9},{2,10},{3,11},{4,12},{5,13},{6,14},{7,15},{8,16},{9,17... | collective-permute-start | bytes 589832 | tf_op jit(solution)/shard_map/ppermute | solution.py:36
  27.6 0.7 %sent_6.1._ = bf16[6,128,128]{2,1,0:T(8,128)(2,1)S(1)} custom-call(f32[24,128,128]{2,1,0:T(8,128)S(1)} %get-tuple-element.13._.base_ref, bf16[384,768]{1,0:T(8,128)(2,1)S(1)} %get-tuple-element.17.spread_ref, bf16[24,128,128]{2,1,0:T(8,128)(2,1)S(1)} %collective-permute-done.raw_ref, bf16[2,128,128]{2,1,0:T(8,128)(2,1)S(1)} %collective-permute-done.1.odd_ref, ...), custom_call_target="tpu_custom_call" | custom-call | flops 2500000000 | bytes 1048576 | tf_op jit(solution)/shard_map/sent_6/pallas_call | solution.py:189
  28.3 3.4 %collective-permute-start.3 = (bf16[6,128,128]{2,1,0:T(8,128)(2,1)S(1)}, bf16[6,128,128]{2,1,0:T(8,128)(2,1)S(1)}, u32[]{:S(2)}, u32[]{:S(2)}) collective-permute-start(bf16[6,128,128]{2,1,0:T(8,128)(2,1)S(1)} %sent_6.1._), channel_id=1, source_target_pairs={{0,8},{1,9},{2,10},{3,11},{4,12},{5,13},{6,14},{7,15},{8,16},{9,17... | collective-permute-start | bytes 589832 | tf_op jit(solution)/shard_map/ppermute | solution.py:36
  31.7 0.7 %sent_12.1._ = bf16[6,128,128]{2,1,0:T(8,128)(2,1)S(1)} custom-call(f32[24,128,128]{2,1,0:T(8,128)S(1)} %get-tuple-element.13._.base_ref, bf16[384,768]{1,0:T(8,128)(2,1)S(1)} %get-tuple-element.17.spread_ref, bf16[24,128,128]{2,1,0:T(8,128)(2,1)S(1)} %collective-permute-done.raw_ref, bf16[2,128,128]{2,1,0:T(8,128)(2,1)S(1)} %collective-permute-done.1.odd_ref, ...), custom_call_target="tpu_custom_call" | custom-call | flops 2500000000 | bytes 1048576 | tf_op jit(solution)/shard_map/sent_12/pallas_call | solution.py:189
  32.4 3.4 %collective-permute-start.4 = (bf16[6,128,128]{2,1,0:T(8,128)(2,1)S(1)}, bf16[6,128,128]{2,1,0:T(8,128)(2,1)S(1)}, u32[]{:S(2)}, u32[]{:S(2)}) collective-permute-start(bf16[6,128,128]{2,1,0:T(8,128)(2,1)S(1)} %sent_12.1._), channel_id=1, source_target_pairs={{0,8},{1,9},{2,10},{3,11},{4,12},{5,13},{6,14},{7,15},{8,16},{9,17... | collective-permute-start | bytes 589832 | tf_op jit(solution)/shard_map/ppermute | solution.py:36
  35.8 1.4 %kept.1.base_ref._ = f32[24,128,128]{2,1,0:T(8,128)S(1)} custom-call(f32[24,128,128]{2,1,0:T(8,128)S(1)} %get-tuple-element.14._.base_ref, bf16[384,768]{1,0:T(8,128)(2,1)S(1)} %get-tuple-element.15.spread_ref, bf16[24,128,128]{2,1,0:T(8,128)(2,1)S(1)} %collective-permute-done.raw_ref, bf16[2,128,128]{2,1,0:T(8,128)(2,1)S(1)} %collective-permute-done.1.odd_ref, ...), custom_call_target="tpu_custom_call" | custom-call | flops 2500000000 | bytes 1048576 | tf_op jit(solution)/shard_map/kept/pallas_call | solution.py:189
  37.2 6.7 %collective-permute-done.2.up_ref = bf16[6,128,128]{2,1,0:T(8,128)(2,1)S(1)} collective-permute-done((bf16[6,128,128]{2,1,0:T(8,128)(2,1)S(1)}, bf16[6,128,128]{2,1,0:T(8,128)(2,1)S(1)}, u32[]{:S(2)}, u32[]{:S(2)}) %collective-permute-start.2) | collective-permute-done | bytes 196640 | tf_op jit(solution)/shard_map/ppermute | solution.py:36
  43.9 1.9 %collective-permute-start.9 = (bf16[6,128,128]{2,1,0:T(8,128)(2,1)S(1)}, bf16[6,128,128]{2,1,0:T(8,128)(2,1)S(1)}, u32[]{:S(2)}, u32[]{:S(2)}) collective-permute-start(bf16[6,128,128]{2,1,0:T(8,128)(2,1)S(1)} %total_0.1._), channel_id=1, source_target_pairs={{0,64},{64,128},{128,192},{192,256},{256,320},{320,384},{384,448},... | collective-permute-start | bytes 589832 | tf_op jit(solution)/shard_map/ppermute | solution.py:36
  45.9 0.7 %sent_18.1._ = bf16[6,128,128]{2,1,0:T(8,128)(2,1)S(1)} custom-call(f32[24,128,128]{2,1,0:T(8,128)S(1)} %get-tuple-element.13._.base_ref, bf16[384,768]{1,0:T(8,128)(2,1)S(1)} %get-tuple-element.17.spread_ref, bf16[24,128,128]{2,1,0:T(8,128)(2,1)S(1)} %collective-permute-done.raw_ref, bf16[2,128,128]{2,1,0:T(8,128)(2,1)S(1)} %collective-permute-done.1.odd_ref, ...), custom_call_target="tpu_custom_call" | custom-call | flops 2500000000 | bytes 1048576 | tf_op jit(solution)/shard_map/sent_18/pallas_call | solution.py:189
  46.6 1.9 %collective-permute-start.5 = (bf16[6,128,128]{2,1,0:T(8,128)(2,1)S(1)}, bf16[6,128,128]{2,1,0:T(8,128)(2,1)S(1)}, u32[]{:S(2)}, u32[]{:S(2)}) collective-permute-start(bf16[6,128,128]{2,1,0:T(8,128)(2,1)S(1)} %sent_18.1._), channel_id=1, source_target_pairs={{0,8},{1,9},{2,10},{3,11},{4,12},{5,13},{6,14},{7,15},{8,16},{9,17... | collective-permute-start | bytes 589832 | tf_op jit(solution)/shard_map/ppermute | solution.py:36
  48.5 0.0 collective-permute-done.3.up_ref
  48.6 3.2 %collective-permute-start.8 = (bf16[6,128,128]{2,1,0:T(8,128)(2,1)S(1)}, bf16[6,128,128]{2,1,0:T(8,128)(2,1)S(1)}, u32[]{:S(2)}, u32[]{:S(2)}) collective-permute-start(bf16[6,128,128]{2,1,0:T(8,128)(2,1)S(1)} %total_6.1._), channel_id=1, source_target_pairs={{0,64},{64,128},{128,192},{192,256},{256,320},{320,384},{384,448},... | collective-permute-start | bytes 589832 | tf_op jit(solution)/shard_map/ppermute | solution.py:36
  51.8 0.0 collective-permute-done.4.up_ref
  51.9 1.9 %collective-permute-start.7 = (bf16[6,128,128]{2,1,0:T(8,128)(2,1)S(1)}, bf16[6,128,128]{2,1,0:T(8,128)(2,1)S(1)}, u32[]{:S(2)}, u32[]{:S(2)}) collective-permute-start(bf16[6,128,128]{2,1,0:T(8,128)(2,1)S(1)} %total_12.1._), channel_id=1, source_target_pairs={{0,64},{64,128},{128,192},{192,256},{256,320},{320,384},{384,448},... | collective-permute-start | bytes 589832 | tf_op jit(solution)/shard_map/ppermute | solution.py:36
  53.8 10.3 %collective-permute-done.5.up_ref = bf16[6,128,128]{2,1,0:T(8,128)(2,1)S(1)} collective-permute-done((bf16[6,128,128]{2,1,0:T(8,128)(2,1)S(1)}, bf16[6,128,128]{2,1,0:T(8,128)(2,1)S(1)}, u32[]{:S(2)}, u32[]{:S(2)}) %collective-permute-start.5) | collective-permute-done | bytes 196640 | tf_op jit(solution)/shard_map/ppermute | solution.py:36
  64.1 2.0 %collective-permute-start.6 = (bf16[6,128,128]{2,1,0:T(8,128)(2,1)S(1)}, bf16[6,128,128]{2,1,0:T(8,128)(2,1)S(1)}, u32[]{:S(2)}, u32[]{:S(2)}) collective-permute-start(bf16[6,128,128]{2,1,0:T(8,128)(2,1)S(1)} %total_18.1), channel_id=1, source_target_pairs={{0,64},{64,128},{128,192},{192,256},{256,320},{320,384},{384,448},... | collective-permute-start | bytes 589832 | tf_op jit(solution)/shard_map/ppermute | solution.py:36
  66.2 0.0 collective-permute-done.9.part_ref
  66.2 0.7 placed_0.1.refs_0_
  66.9 0.0 collective-permute-done.8.part_ref
  66.9 0.7 placed_6.1.refs_0_
  67.6 0.0 collective-permute-done.7.part_ref
  67.6 0.7 placed_12.1.refs_0_
  68.3 1.0 %maximum_bitcast_fusion = bf16[1,1,24,128,128]{4,3,2,1,0:T(8,128)(2,1)} fusion(bf16[6,128,128]{2,1,0:T(8,128)(2,1)S(1)} %total_18.1, bf16[6,128,128]{2,1,0:T(8,128)(2,1)S(1)} %total_12.1._, bf16[6,128,128]{2,1,0:T(8,128)(2,1)S(1)} %total_6.1._, bf16[6,128,128]{2,1,0:T(8,128)(2,1)S(1)} %total_0.1._), kind=kLoop, calls=%fused_computation | loop fusion | flops 1179648 | bytes 1572864 | tf_op jit(solution)/shard_map/broadcast_in_dim | solution.py:269
  69.3 1.9 %collective-permute-done.6.part_ref = bf16[6,128,128]{2,1,0:T(8,128)(2,1)S(1)} collective-permute-done((bf16[6,128,128]{2,1,0:T(8,128)(2,1)S(1)}, bf16[6,128,128]{2,1,0:T(8,128)(2,1)S(1)}, u32[]{:S(2)}, u32[]{:S(2)}) %collective-permute-start.6) | collective-permute-done | bytes 196640 | tf_op jit(solution)/shard_map/ppermute | solution.py:36
  71.1 0.7 placed_18.1
  (4 shorter events, 0.1 us)
Async XLA Ops:
  0.6 22.8 %collective-permute-start = (bf16[24,128,128]{2,1,0:T(8,128)(2,1)}, bf16[24,128,128]{2,1,0:T(8,128)(2,1)S(1)}, u32[]{:S(2)}, u32[]{:S(2)}) collective-permute-start(bf16[24,128,128]{2,1,0:T(8,128)(2,1)} %bitcast.6), channel_id=1, source_target_pairs={{0,1},{1,2},{2,3},{3,4},{4,5},{5,6},{6,7},{8,9},{9,10},{10,11},{11... | collective-permute-start | bytes 2359304 | tf_op jit(solution)/shard_map/ppermute | solution.py:36
  3.2 20.2 %collective-permute-start.1 = (bf16[2,128,128]{2,1,0:T(8,128)(2,1)S(1)}, bf16[2,128,128]{2,1,0:T(8,128)(2,1)S(1)}, u32[]{:S(2)}, u32[]{:S(2)}) collective-permute-start(bf16[2,128,128]{2,1,0:T(8,128)(2,1)S(1)} %get-tuple-element.16), channel_id=1, source_target_pairs={{0,1},{1,2},{2,3},{3,4},{4,5},{5,6},{6,7},{8,9},{9,10},{10,11},{11... | collective-permute-start | bytes 196616 | tf_op jit(solution)/shard_map/ppermute | solution.py:36
  24.2 19.7 %collective-permute-start.2 = (bf16[6,128,128]{2,1,0:T(8,128)(2,1)S(1)}, bf16[6,128,128]{2,1,0:T(8,128)(2,1)S(1)}, u32[]{:S(2)}, u32[]{:S(2)}) collective-permute-start(bf16[6,128,128]{2,1,0:T(8,128)(2,1)S(1)} %sent_0.1._), channel_id=1, source_target_pairs={{0,8},{1,9},{2,10},{3,11},{4,12},{5,13},{6,14},{7,15},{8,16},{9,17... | collective-permute-start | bytes 589832 | tf_op jit(solution)/shard_map/ppermute | solution.py:36
  28.3 20.2 %collective-permute-start.3 = (bf16[6,128,128]{2,1,0:T(8,128)(2,1)S(1)}, bf16[6,128,128]{2,1,0:T(8,128)(2,1)S(1)}, u32[]{:S(2)}, u32[]{:S(2)}) collective-permute-start(bf16[6,128,128]{2,1,0:T(8,128)(2,1)S(1)} %sent_6.1._), channel_id=1, source_target_pairs={{0,8},{1,9},{2,10},{3,11},{4,12},{5,13},{6,14},{7,15},{8,16},{9,17... | collective-permute-start | bytes 589832 | tf_op jit(solution)/shard_map/ppermute | solution.py:36
  32.4 19.4 %collective-permute-start.4 = (bf16[6,128,128]{2,1,0:T(8,128)(2,1)S(1)}, bf16[6,128,128]{2,1,0:T(8,128)(2,1)S(1)}, u32[]{:S(2)}, u32[]{:S(2)}) collective-permute-start(bf16[6,128,128]{2,1,0:T(8,128)(2,1)S(1)} %sent_12.1._), channel_id=1, source_target_pairs={{0,8},{1,9},{2,10},{3,11},{4,12},{5,13},{6,14},{7,15},{8,16},{9,17... | collective-permute-start | bytes 589832 | tf_op jit(solution)/shard_map/ppermute | solution.py:36
  43.9 22.3 %collective-permute-start.9 = (bf16[6,128,128]{2,1,0:T(8,128)(2,1)S(1)}, bf16[6,128,128]{2,1,0:T(8,128)(2,1)S(1)}, u32[]{:S(2)}, u32[]{:S(2)}) collective-permute-start(bf16[6,128,128]{2,1,0:T(8,128)(2,1)S(1)} %total_0.1._), channel_id=1, source_target_pairs={{0,64},{64,128},{128,192},{192,256},{256,320},{320,384},{384,448},... | collective-permute-start | bytes 589832 | tf_op jit(solution)/shard_map/ppermute | solution.py:36
  46.6 17.5 %collective-permute-start.5 = (bf16[6,128,128]{2,1,0:T(8,128)(2,1)S(1)}, bf16[6,128,128]{2,1,0:T(8,128)(2,1)S(1)}, u32[]{:S(2)}, u32[]{:S(2)}) collective-permute-start(bf16[6,128,128]{2,1,0:T(8,128)(2,1)S(1)} %sent_18.1._), channel_id=1, source_target_pairs={{0,8},{1,9},{2,10},{3,11},{4,12},{5,13},{6,14},{7,15},{8,16},{9,17... | collective-permute-start | bytes 589832 | tf_op jit(solution)/shard_map/ppermute | solution.py:36
  48.6 18.3 %collective-permute-start.8 = (bf16[6,128,128]{2,1,0:T(8,128)(2,1)S(1)}, bf16[6,128,128]{2,1,0:T(8,128)(2,1)S(1)}, u32[]{:S(2)}, u32[]{:S(2)}) collective-permute-start(bf16[6,128,128]{2,1,0:T(8,128)(2,1)S(1)} %total_6.1._), channel_id=1, source_target_pairs={{0,64},{64,128},{128,192},{192,256},{256,320},{320,384},{384,448},... | collective-permute-start | bytes 589832 | tf_op jit(solution)/shard_map/ppermute | solution.py:36
  51.9 15.7 %collective-permute-start.7 = (bf16[6,128,128]{2,1,0:T(8,128)(2,1)S(1)}, bf16[6,128,128]{2,1,0:T(8,128)(2,1)S(1)}, u32[]{:S(2)}, u32[]{:S(2)}) collective-permute-start(bf16[6,128,128]{2,1,0:T(8,128)(2,1)S(1)} %total_12.1._), channel_id=1, source_target_pairs={{0,64},{64,128},{128,192},{192,256},{256,320},{320,384},{384,448},... | collective-permute-start | bytes 589832 | tf_op jit(solution)/shard_map/ppermute | solution.py:36
  64.1 7.0 %collective-permute-start.6 = (bf16[6,128,128]{2,1,0:T(8,128)(2,1)S(1)}, bf16[6,128,128]{2,1,0:T(8,128)(2,1)S(1)}, u32[]{:S(2)}, u32[]{:S(2)}) collective-permute-start(bf16[6,128,128]{2,1,0:T(8,128)(2,1)S(1)} %total_18.1), channel_id=1, source_target_pairs={{0,64},{64,128},{128,192},{192,256},{256,320},{320,384},{384,448},... | collective-permute-start | bytes 589832 | tf_op jit(solution)/shard_map/ppermute | solution.py:36

commit v3 on v2

v3 whole, which is shorter than its diff:
```python
import functools

import jax
import jax.numpy as jnp
from jax import lax
from jax.experimental import pallas as pl
from jax.experimental.pallas import tpu as pltpu
from jax.sharding import PartitionSpec as P

STATES = 4
CHARGES = 8
BLOCK = 128
CHANNELS = 24
SECTORS = 64
TILE = 16
ROWS = CHANNELS * TILE
CARRY = 3
PLAIN = (0, 1, 2, 4, 5, 6)
HEAD = 18
TAIL = CHANNELS - HEAD
CUTS = (0, 12, 24)
HANDED = ((0,), (1,))
CHUNKS = tuple(zip(CUTS[:-1], CUTS[1:]))
VMEM = pl.BlockSpec(memory_space=pltpu.VMEM)
SMEM = pl.BlockSpec(memory_space=pltpu.SMEM)
HBM = pl.BlockSpec(memory_space=pltpu.HBM)
ANY = pl.BlockSpec(memory_space=pl.ANY)
PARAMS = pltpu.CompilerParams(vmem_limit_bytes=32 * 1024 * 1024)
MIXED = pltpu.VMEM((CHANNELS, BLOCK, BLOCK), jnp.bfloat16)


def array(dtype, *shape):
    return jax.ShapeDtypeStruct(shape, dtype)


def send(shard, axis, by, charges=range(CHARGES)):
    devices = lax.axis_size(axis)
    pairs = [(i, i + by) for i in range(devices) if 0 <= i + by < devices]
    if axis == "sec":
        pairs = [(i, j) for i, j in pairs if i % CHARGES in charges]
    return lax.ppermute(shard, axis, pairs)


def two_terms(x):
    high = x.astype(jnp.bfloat16)
    low = (x - high.astype(jnp.float32)).astype(jnp.bfloat16)
    return high, low


def spread_weights(weights, low, high):
    rows = (high - low) * TILE
    channel_of_row = lax.broadcasted_iota(jnp.int32, (rows, CHANNELS), 0) // TILE + low
    pick_c = (channel_of_row == lax.broadcasted_iota(jnp.int32, (rows, CHANNELS), 1)).astype(jnp.bfloat16)
    channel_of_row = lax.broadcasted_iota(jnp.int32, (ROWS, CHANNELS), 0) // TILE
    pick_b = (channel_of_row == lax.broadcasted_iota(jnp.int32, (ROWS, CHANNELS), 1)).astype(jnp.bfloat16)
    row = lax.broadcasted_iota(jnp.int32, (rows, ROWS), 0) % TILE
    col = lax.broadcasted_iota(jnp.int32, (rows, ROWS), 1) % TILE
    same = row == col
    contract = (((1,), (1,)), ((), ()))
    parts = []
    for term in two_terms(weights):
        by_row = lax.dot_general(pick_c, term, contract, preferred_element_type=jnp.float32)
        full = lax.dot_general(by_row.astype(jnp.bfloat16), pick_b, contract, preferred_element_type=jnp.float32)
        parts.append(jnp.where(same, full, 0.0).astype(jnp.bfloat16))
    return jnp.concatenate(parts, axis=1)


def update(cur_refs, block, spread, count, mixed_ref, emit):
    def rows_at(at):
        parts = [ref[:, at : at + TILE, :].reshape(ref.shape[0] * TILE, BLOCK) for ref in cur_refs]
        return parts[0] if len(parts) == 1 else jnp.concatenate(parts, axis=0)

    for first in range(0, BLOCK, 2 * TILE):
        left, right = rows_at(first), rows_at(first + TILE)
        both = jnp.concatenate([left, right], axis=1)
        both = jnp.concatenate([both, both], axis=0)
        mixed = jnp.dot(spread, both, preferred_element_type=jnp.float32).astype(jnp.bfloat16)
        for half in range(2):
            at = first + half * TILE
            mixed_ref[:count, at : at + TILE, :] = mixed[:, half * BLOCK : (half + 1) * BLOCK].reshape(count, TILE, BLOCK)
    left_block = block.astype(jnp.float32).T.astype(jnp.bfloat16)
    left_block = jnp.concatenate([left_block, left_block], axis=1)
    for c in range(0, count, 2):
        rows = mixed_ref[c : c + 2].reshape(2 * BLOCK, BLOCK)
        high, low = two_terms(jnp.dot(rows, block, preferred_element_type=jnp.float32))
        first = jnp.concatenate([high[:BLOCK], high[BLOCK:]], axis=1)
        second = jnp.concatenate([low[:BLOCK], low[BLOCK:]], axis=1)
        pairs = jnp.concatenate([first, second], axis=0)
        result = jnp.dot(left_block, pairs, preferred_element_type=jnp.float32)
        emit(c, result[:, :BLOCK])
        emit(c + 1, result[:, BLOCK:])


def masked(block, rows, cols):
    row = lax.broadcasted_iota(jnp.int32, (BLOCK, BLOCK), 0)
    col = lax.broadcasted_iota(jnp.int32, (BLOCK, BLOCK), 1)
    return jnp.where((row < rows) & (col < cols), block.astype(jnp.float32), 0.0).astype(jnp.bfloat16)


def loaded_kernel(sizes_hbm, cur_hbm, tensors_hbm, couplings_hbm, pattern_hbm, *refs):
    parcel_ref, even_ref, head_ref, tail_ref, weights_ref, sizes_ref, tensors_ref, pattern_ref, sems = refs
    copies = [
        pltpu.make_async_copy(source, target, sems.at[at])
        for at, (source, target) in enumerate(
            (
                (sizes_hbm, sizes_ref),
                (tensors_hbm, tensors_ref),
                (couplings_hbm, weights_ref),
                (pattern_hbm, pattern_ref),
                (cur_hbm, parcel_ref.at[:CHANNELS]),
                (cur_hbm.at[:HEAD], head_ref),
                (cur_hbm.at[HEAD:], tail_ref.at[:TAIL]),
            )
        )
    ]
    for copy in copies:
        copy.start()
    copies[0].wait()
    copies[1].wait()
    sector = lax.axis_index("sec")
    for state in range(STATES):
        target = jnp.minimum(sector + state // 2 * CHARGES + state % 2, SECTORS - 1)
        block = masked(tensors_ref[state], sizes_ref[sector], sizes_ref[target])
        if state % 2:
            parcel_ref[CHANNELS + state // 2] = block
            tail_ref[TAIL + state // 2] = block
        else:
            even_ref[state // 2] = block
    copies[2].wait()
    copies[3].wait()
    pattern = pattern_ref[...].astype(jnp.float32)
    for state in range(STATES):
        weights_ref[state] = weights_ref[state] * pattern
    for copy in copies[4:]:
        copy.wait()


COSTS = dict(
    loaded=1, first=1, own_2=0.01, own_0=0.01, kept=1,
    **{f"{kind}_{low}": 10 if low < CUTS[-2] else 1 for kind in ("total", "placed") for low in CUTS},
    **{f"sent_{low}": 1 if low else 10 for low in CUTS},
)


def cost(name):
    return pl.CostEstimate(flops=int(COSTS[name] * 2.5e9), bytes_accessed=1 << 20, transcendentals=0)


def loaded(sizes, cur, tensors, couplings, pattern):
    stay = [pltpu.with_memory_space_constraint(x, pltpu.HBM) for x in (sizes, cur, tensors, couplings, pattern)]
    return pl.pallas_call(
        loaded_kernel,
        out_shape=(
            array(jnp.bfloat16, CHANNELS + 2, BLOCK, BLOCK),
            array(jnp.bfloat16, 2, BLOCK, BLOCK),
            array(jnp.bfloat16, HEAD, BLOCK, BLOCK),
            array(jnp.bfloat16, TAIL + 2, BLOCK, BLOCK),
            array(jnp.float32, STATES, CHANNELS, CHANNELS),
        ),
        in_specs=[HBM] * 5,
        out_specs=(VMEM,) * 5,
        scratch_shapes=[
            pltpu.SMEM((SECTORS,), jnp.int32),
            pltpu.VMEM((STATES, BLOCK, BLOCK), jnp.bfloat16),
            pltpu.VMEM((CHANNELS, CHANNELS), jnp.int32),
            pltpu.SemaphoreType.DMA((7,)),
        ],
        compiler_params=PARAMS,
        cost_estimate=cost("loaded"),
        name="loaded",
    )(*stay)


def first_kernel(parcel_ref, weights_ref, out_ref, mixed_ref):
    def emit(c, value):
        out_ref[c] = value.astype(out_ref.dtype)

    low, high = CHUNKS[0]
    spread = spread_weights(weights_ref[3], low, high)
    update([parcel_ref.at[:CHANNELS]], parcel_ref[CHANNELS + 1], spread, high - low, mixed_ref, emit)


def first(parcel, weights):
    low, high = CHUNKS[0]
    return pl.pallas_call(
        first_kernel,
        out_shape=array(jnp.bfloat16, high - low, BLOCK, BLOCK),
        in_specs=[VMEM] * 2,
        out_specs=VMEM,
        scratch_shapes=[MIXED],
        compiler_params=PARAMS,
        cost_estimate=cost("first"),
        name="first",
    )(parcel, weights)


def own_kernel(state, again, cur_ref, even_ref, weights_ref, _, out_ref, spread_ref, *refs):
    *later_refs, mixed_ref, sem = refs

    def emit(c, value):
        out_ref[c] = value

    copies = [pltpu.make_async_copy(cur_ref, ref, sem) for ref in later_refs]
    for copy in copies:
        copy.start()
    spread = spread_weights(weights_ref[state], 0, CHANNELS)
    update([cur_ref.at[:CHANNELS]], even_ref[state // 2], spread, CHANNELS, mixed_ref, emit)
    spread_ref[...] = spread_weights(weights_ref[state + 1], 0, CHANNELS)
    for copy in copies:
        copy.wait()


def own(state, again, cur, even, weights, after):
    name = f"own_{state}"
    return pl.pallas_call(
        functools.partial(own_kernel, state, again),
        out_shape=(
            array(jnp.float32, CHANNELS, BLOCK, BLOCK),
            array(jnp.bfloat16, ROWS, 2 * ROWS),
            *(array(cur.dtype, *cur.shape),) * again,
        ),
        in_specs=[VMEM] * 3 + [ANY],
        out_specs=(VMEM,) * (2 + again),
        scratch_shapes=[MIXED, pltpu.SemaphoreType.DMA],
        compiler_params=PARAMS,
        cost_estimate=cost(name),
        name=name,
    )(cur, even, weights, after)


def joined_kernel(state, low, high, came, base_ref, spread_ref, head_ref, tail_ref, plain_ref, _, out_ref, mixed_ref):
    carried = lax.rem(lax.axis_index("sec"), CHARGES) == CARRY + 1

    def work_out(cur_refs, block):
        def emit(c, value):
            out_ref[c] = (base_ref[low + c] + value).astype(out_ref.dtype)

        update(cur_refs, block, spread_ref[low * TILE : high * TILE, :], high - low, mixed_ref, emit)

    @pl.when(carried)
    def _():
        work_out([head_ref, tail_ref.at[:TAIL]], tail_ref[TAIL + state // 2])

    @pl.when(jnp.logical_not(carried))
    def _():
        if came:
            out_ref[...] = (base_ref[low:high] + plain_ref[...].astype(jnp.float32)).astype(out_ref.dtype)
        else:
            work_out([plain_ref.at[:CHANNELS]], plain_ref[CHANNELS + state // 2])


def joined(name, state, low, high, came, dtype, base, spread, head, tail, plain, after):
    return pl.pallas_call(
        functools.partial(joined_kernel, state, low, high, came),
        out_shape=array(dtype, high - low, BLOCK, BLOCK),
        in_specs=[VMEM] * 5 + [ANY],
        out_specs=VMEM,
        scratch_shapes=[MIXED],
        compiler_params=PARAMS,
        cost_estimate=cost(name),
        name=name,
    )(base, spread, head, tail, plain, after)


def total_kernel(low, kept_ref, *refs):
    *part_refs, _, out_ref = refs
    at = 0
    for part_ref in part_refs:
        end = at + part_ref.shape[0]
        out_ref[at:end] = (kept_ref[low + at : low + end] + part_ref[...].astype(jnp.float32)).astype(jnp.bfloat16)
        at = end


def total(low, high, kept, parts, after):
    return pl.pallas_call(
        functools.partial(total_kernel, low),
        out_shape=array(jnp.bfloat16, high - low, BLOCK, BLOCK),
        in_specs=[VMEM] * (1 + len(parts)) + [ANY],
        out_specs=VMEM,
        compiler_params=PARAMS,
        cost_estimate=cost(f"total_{low}"),
        name=f"total_{low}",
    )(kept, *parts, after)


def placed_kernel(low, high, done_ref, came_ref, *refs):
    whole_hbm, handed_hbm, sems = refs[-3:]
    copies = [
        pltpu.make_async_copy(done_ref, whole_hbm.at[low:high], sems.at[0]),
        pltpu.make_async_copy(came_ref, handed_hbm.at[low:high], sems.at[1]),
    ]
    for copy in copies:
        copy.start()
    for copy in copies:
        copy.wait()


def placed(wholes, low, high, done, came):
    whole = array(done.dtype, CHANNELS, BLOCK, BLOCK)
    return pl.pallas_call(
        functools.partial(placed_kernel, low, high),
        out_shape=(whole, whole),
        in_specs=[VMEM] * 2 + [HBM] * len(wholes),
        out_specs=(HBM, HBM),
        scratch_shapes=[pltpu.SemaphoreType.DMA((2,))],
        input_output_aliases={2: 0, 3: 1} if wholes else {},
        compiler_params=PARAMS,
        cost_estimate=cost(f"placed_{low}"),
        name=f"placed_{low}",
    )(done, came, *wholes)


def per_device(site_tensors, boundary, couplings, pattern, sizes):
    parcel, even, head, tail, weights = loaded(sizes, boundary[0, 0], site_tensors[0, 0], couplings[0], pattern)
    head = send(head, "sec", 1, (CARRY,))
    tail = send(tail, "sec", -CARRY, (CARRY,))
    tail = send(tail, "sec", CARRY + 1, (0,))
    sent = first(parcel, weights)
    came = send(sent, "sec", 1, PLAIN)
    up, spread_up, later = own(2, 1, parcel, even, weights, sent)
    plain = send(later, "sec", 1, PLAIN)
    kept, spread_kept = own(0, 0, parcel, even, weights, up)
    arrived, last = [], kept
    for low, high in CHUNKS:
        here = plain if low else came
        last = joined(f"sent_{low}", 3, low, high, not low, jnp.bfloat16, up, spread_up, head, tail, here, last)
        arrived.append(send(last, "sec", CHARGES))
    kept = last = joined("kept", 1, 0, CHANNELS, False, jnp.float32, kept, spread_kept, head, tail, plain, last)
    waiting, wholes = [], ()
    for chunks in HANDED:
        low, high = CUTS[chunks[0]], CUTS[chunks[-1] + 1]
        last = total(low, high, kept, [arrived[at] for at in chunks], last)
        waiting.append((low, high, last, send(last, "seg", 1)))
    for parts in waiting:
        wholes = placed(wholes, *parts)
    return tuple(whole[None, None] for whole in wholes)


def solution(mesh):
    return jax.shard_map(
        per_device,
        mesh=mesh,
        in_specs=(
            P("seg", "sec", None, None, None),
            P("seg", "sec", None, None, None),
            P("seg", None, None, None),
            P(),
            P(),
        ),
        out_specs=(P("seg", "sec", None, None, None), P("seg", "sec", None, None, None)),
        check_vma=False,
    )
```

time: 72.2 us -> 70.1 us (0.971)
  the two profiles are of different devices: /device:TPU:316 before, /device:TPU:134 now
where the time goes in v3:
time: 70.1 us; the launch traced here: 69.8 us
  waiting for transfers between devices  36 us (51%)
  starting transfers between devices  21.7 us (31%)
  Pallas kernels  11.3 us (16%)
  between operations  0.82 us (1%)
    ppermute x9, waiting for transfers between devices, send(): return lax.ppermute(shard, axis, pairs)  36 us
    ppermute x9, starting transfers between devices, send(): return lax.ppermute(shard, axis, pairs)  21.7 us
    pallas_call x2, Pallas kernels, own(): pl.pallas_call(functools.partial(own_kernel, state, again), out_shape=(ar...  4.18 us
    pallas_call x3, Pallas kernels, joined(): pl.pallas_call(functools.partial(joined_kernel, state, low, high, came),...  2.4 us
    pallas_call x2, Pallas kernels, placed(): pl.pallas_call(functools.partial(placed_kernel, low, high), out_shape=(wh...  1.79 us
    pallas_call x1, Pallas kernels, loaded(): pl.pallas_call(loaded_kernel, out_shape=(array(jnp.bfloat16, CHANNELS + 2...  1.54 us
  transfers between devices with their start and end apart: 9, of which 4 were waited for; matrix products, arithmetic and copies ran while one was open for 0% of the time, Pallas kernels for 13%

profile of v3, /device:TPU:134, one launch (start us, length us, event | category | flops | bytes accessed | tf_op | source)
XLA Modules:
  0.0 69.8 jit_solution(17779197576175034229)
XLA Ops:
  0.6 1.5 %loaded.1 = (bf16[26,128,128]{2,1,0:T(8,128)(2,1)S(1)}, bf16[2,128,128]{2,1,0:T(8,128)(2,1)S(1)}, bf16[18,128,128]{2,1,0:T(8,128)(2,1)S(1)}, bf16[8,128,128]{2,1,0:T(8,128)(2,1)S(1)}, f32[4,24,24]{2,1,0:T(8,128)S(1)}) custom-call(s32[64]{0:T(128)} %sizes_hbm.1, bf16[24,128,128]{2,1,0:T(8,128)(2,1)} %bitcast.5, bf16[4,128,128]{2,1,0:T(8,128)(2,1)} %bitcast.6, ...), custom_call_target="tpu_custom_call" | custom-call | flops 2500000000 | bytes 1048576 | tf_op jit(solution)/shard_map/loaded/pallas_call | solution.py:151
  2.2 1.3 %collective-permute-start.1 = (bf16[8,128,128]{2,1,0:T(8,128)(2,1)S(1)}, bf16[8,128,128]{2,1,0:T(8,128)(2,1)S(1)}, u32[]{:S(2)}, u32[]{:S(2)}) collective-permute-start(bf16[8,128,128]{2,1,0:T(8,128)(2,1)S(1)} %get-tuple-element.23), channel_id=1, source_target_pairs={{3,0},{11,8},{19,16},{27,24},{35,32},{43,40},{51,48},{59,56},{67,6... | collective-permute-start | bytes 786440 | tf_op jit(solution)/shard_map/ppermute | solution.py:41
  3.5 0.7 %collective-permute-start = (bf16[18,128,128]{2,1,0:T(8,128)(2,1)S(1)}, bf16[18,128,128]{2,1,0:T(8,128)(2,1)S(1)}, u32[]{:S(2)}, u32[]{:S(2)}) collective-permute-start(bf16[18,128,128]{2,1,0:T(8,128)(2,1)S(1)} %get-tuple-element.22), channel_id=1, source_target_pairs={{3,4},{11,12},{19,20},{27,28},{35,36},{43,44},{51,52},{59,60},{67,... | collective-permute-start | bytes 1769480 | tf_op jit(solution)/shard_map/ppermute | solution.py:41
  4.2 1.2 %first.1._ = bf16[12,128,128]{2,1,0:T(8,128)(2,1)S(1)} custom-call(bf16[26,128,128]{2,1,0:T(8,128)(2,1)S(1)} %get-tuple-element.16.parcel_ref.cur_ref, f32[4,24,24]{2,1,0:T(8,128)S(1)} %get-tuple-element.18.weights_ref), custom_call_target="tpu_custom_call" | custom-call | flops 2500000000 | bytes 1048576 | tf_op jit(solution)/shard_map/first/pallas_call | solution.py:185
  5.4 2.9 %collective-permute-start.4 = (bf16[12,128,128]{2,1,0:T(8,128)(2,1)S(1)}, bf16[12,128,128]{2,1,0:T(8,128)(2,1)S(1)}, u32[]{:S(2)}, u32[]{:S(2)}) collective-permute-start(bf16[12,128,128]{2,1,0:T(8,128)(2,1)S(1)} %first.1._), channel_id=1, source_target_pairs={{0,1},{1,2},{2,3},{4,5},{5,6},{6,7},{8,9},{9,10},{10,11},{12,13},{... | collective-permute-start | bytes 1179656 | tf_op jit(solution)/shard_map/ppermute | solution.py:41
  8.3 5.0 %collective-permute-done.1 = bf16[8,128,128]{2,1,0:T(8,128)(2,1)S(1)} collective-permute-done((bf16[8,128,128]{2,1,0:T(8,128)(2,1)S(1)}, bf16[8,128,128]{2,1,0:T(8,128)(2,1)S(1)}, u32[]{:S(2)}, u32[]{:S(2)}) %collective-permute-start.1) | collective-permute-done | bytes 262176 | tf_op jit(solution)/shard_map/ppermute | solution.py:41
  13.3 1.3 %collective-permute-start.2 = (bf16[8,128,128]{2,1,0:T(8,128)(2,1)S(1)}, bf16[8,128,128]{2,1,0:T(8,128)(2,1)S(1)}, u32[]{:S(2)}, u32[]{:S(2)}) collective-permute-start(bf16[8,128,128]{2,1,0:T(8,128)(2,1)S(1)} %collective-permute-done.1), channel_id=1, source_target_pairs={{0,4},{8,12},{16,20},{24,28},{32,36},{40,44},{48,52},{56,60},{64,6... | collective-permute-start | bytes 786440 | tf_op jit(solution)/shard_map/ppermute | solution.py:41
  14.6 2.2 %own_2.1 = (f32[24,128,128]{2,1,0:T(8,128)S(1)}, bf16[384,768]{1,0:T(8,128)(2,1)S(1)}, bf16[26,128,128]{2,1,0:T(8,128)(2,1)S(1)}) custom-call(bf16[26,128,128]{2,1,0:T(8,128)(2,1)S(1)} %get-tuple-element.16.parcel_ref.cur_ref, bf16[2,128,128]{2,1,0:T(8,128)(2,1)S(1)} %get-tuple-element.17.even_ref, f32[4,24,24]{2,1,0:T(8,128)S(1)} %get-tuple-element.18.weights_ref, ...), custom_call_target="tpu_custom_call" | custom-call | flops 25000000 | bytes 1048576 | tf_op jit(solution)/shard_map/own_2/pallas_call | solution.py:215
  16.8 1.3 %collective-permute-start.3 = (bf16[26,128,128]{2,1,0:T(8,128)(2,1)S(1)}, bf16[26,128,128]{2,1,0:T(8,128)(2,1)S(1)}, u32[]{:S(2)}, u32[]{:S(2)}) collective-permute-start(bf16[26,128,128]{2,1,0:T(8,128)(2,1)S(1)} %get-tuple-element.24), channel_id=1, source_target_pairs={{0,1},{1,2},{2,3},{4,5},{5,6},{6,7},{8,9},{9,10},{10,11},{12,13},{... | collective-permute-start | bytes 2555912 | tf_op jit(solution)/shard_map/ppermute | solution.py:41
  18.2 2.0 %own_0.1 = (f32[24,128,128]{2,1,0:T(8,128)S(1)}, bf16[384,768]{1,0:T(8,128)(2,1)S(1)}) custom-call(bf16[26,128,128]{2,1,0:T(8,128)(2,1)S(1)} %get-tuple-element.16.parcel_ref.cur_ref, bf16[2,128,128]{2,1,0:T(8,128)(2,1)S(1)} %get-tuple-element.17.even_ref, f32[4,24,24]{2,1,0:T(8,128)S(1)} %get-tuple-element.18.weights_ref, ...), custom_call_target="tpu_custom_call" | custom-call | flops 25000000 | bytes 1048576 | tf_op jit(solution)/shard_map/own_0/pallas_call | solution.py:215
  20.2 0.0 collective-permute-done.4.plain_ref
  20.2 0.0 collective-permute-done.2.tail_ref
  20.2 0.0 collective-permute-done.head_ref
  20.2 0.1 sent_0.1._
  20.3 5.2 %collective-permute-start.6 = (bf16[12,128,128]{2,1,0:T(8,128)(2,1)S(1)}, bf16[12,128,128]{2,1,0:T(8,128)(2,1)S(1)}, u32[]{:S(2)}, u32[]{:S(2)}) collective-permute-start(bf16[12,128,128]{2,1,0:T(8,128)(2,1)S(1)} %sent_0.1._), channel_id=1, source_target_pairs={{0,8},{1,9},{2,10},{3,11},{4,12},{5,13},{6,14},{7,15},{8,16},{9,17... | collective-permute-start | bytes 1179656 | tf_op jit(solution)/shard_map/ppermute | solution.py:41
  25.5 10.2 %collective-permute-done.3.plain_ref = bf16[26,128,128]{2,1,0:T(8,128)(2,1)S(1)} collective-permute-done((bf16[26,128,128]{2,1,0:T(8,128)(2,1)S(1)}, bf16[26,128,128]{2,1,0:T(8,128)(2,1)S(1)}, u32[]{:S(2)}, u32[]{:S(2)}) %collective-permute-start.3) | collective-permute-done | bytes 852000 | tf_op jit(solution)/shard_map/ppermute | solution.py:41
  35.7 0.9 %sent_12.1._ = bf16[12,128,128]{2,1,0:T(8,128)(2,1)S(1)} custom-call(f32[24,128,128]{2,1,0:T(8,128)S(1)} %get-tuple-element.19._.base_ref, bf16[384,768]{1,0:T(8,128)(2,1)S(1)} %get-tuple-element.25.spread_ref, bf16[18,128,128]{2,1,0:T(8,128)(2,1)S(1)} %collective-permute-done.head_ref, bf16[8,128,128]{2,1,0:T(8,128)(2,1)S(1)} %collective-permute-done.2.tail_ref, ...), custom_call_target="tpu_custom_call" | custom-call | flops 2500000000 | bytes 1048576 | tf_op jit(solution)/shard_map/sent_12/pallas_call | solution.py:253
  36.6 5.2 %collective-permute-start.5 = (bf16[12,128,128]{2,1,0:T(8,128)(2,1)S(1)}, bf16[12,128,128]{2,1,0:T(8,128)(2,1)S(1)}, u32[]{:S(2)}, u32[]{:S(2)}) collective-permute-start(bf16[12,128,128]{2,1,0:T(8,128)(2,1)S(1)} %sent_12.1._), channel_id=1, source_target_pairs={{0,8},{1,9},{2,10},{3,11},{4,12},{5,13},{6,14},{7,15},{8,16},{9,17... | collective-permute-start | bytes 1179656 | tf_op jit(solution)/shard_map/ppermute | solution.py:41
  41.8 1.4 %kept.1.kept_ref.refs_1_ = f32[24,128,128]{2,1,0:T(8,128)S(1)} custom-call(f32[24,128,128]{2,1,0:T(8,128)S(1)} %get-tuple-element.20._.base_ref, bf16[384,768]{1,0:T(8,128)(2,1)S(1)} %get-tuple-element.21.spread_ref, bf16[18,128,128]{2,1,0:T(8,128)(2,1)S(1)} %collective-permute-done.head_ref, bf16[8,128,128]{2,1,0:T(8,128)(2,1)S(1)} %collective-permute-done.2.tail_ref, ...), custom_call_target="tpu_custom_call" | custom-call | flops 2500000000 | bytes 1048576 | tf_op jit(solution)/shard_map/kept/pallas_call | solution.py:253
  43.2 0.0 collective-permute-done.6.refs_0_
  43.2 0.1 total_0.1.refs_1_.done_ref
  43.3 1.9 %collective-permute-start.8 = (bf16[12,128,128]{2,1,0:T(8,128)(2,1)S(1)}, bf16[12,128,128]{2,1,0:T(8,128)(2,1)S(1)}, u32[]{:S(2)}, u32[]{:S(2)}) collective-permute-start(bf16[12,128,128]{2,1,0:T(8,128)(2,1)S(1)} %total_0.1.refs_1_.done_ref), channel_id=1, source_target_pairs={{0,64},{64,128},{128,192},{192,256},{256,320},{320,384},{384,448},... | collective-permute-start | bytes 1179656 | tf_op jit(solution)/shard_map/ppermute | solution.py:41
  45.2 14.5 %collective-permute-done.5.refs_0_ = bf16[12,128,128]{2,1,0:T(8,128)(2,1)S(1)} collective-permute-done((bf16[12,128,128]{2,1,0:T(8,128)(2,1)S(1)}, bf16[12,128,128]{2,1,0:T(8,128)(2,1)S(1)}, u32[]{:S(2)}, u32[]{:S(2)}) %collective-permute-start.5) | collective-permute-done | bytes 393248 | tf_op jit(solution)/shard_map/ppermute | solution.py:41
  59.8 0.1 total_12.1.done_ref
  59.8 1.9 %collective-permute-start.7 = (bf16[12,128,128]{2,1,0:T(8,128)(2,1)S(1)}, bf16[12,128,128]{2,1,0:T(8,128)(2,1)S(1)}, u32[]{:S(2)}, u32[]{:S(2)}) collective-permute-start(bf16[12,128,128]{2,1,0:T(8,128)(2,1)S(1)} %total_12.1.done_ref), channel_id=1, source_target_pairs={{0,64},{64,128},{128,192},{192,256},{256,320},{320,384},{384,448},... | collective-permute-start | bytes 1179656 | tf_op jit(solution)/shard_map/ppermute | solution.py:41
  61.8 0.0 collective-permute-done.8.came_ref
  61.8 0.9 %placed_0.1 = (bf16[24,128,128]{2,1,0:T(8,128)(2,1)}, bf16[24,128,128]{2,1,0:T(8,128)(2,1)}) custom-call(bf16[12,128,128]{2,1,0:T(8,128)(2,1)S(1)} %total_0.1.refs_1_.done_ref, bf16[12,128,128]{2,1,0:T(8,128)(2,1)S(1)} %collective-permute-done.8.came_ref), custom_call_target="tpu_custom_call" | custom-call | flops 24999999488 | bytes 1048576 | tf_op jit(solution)/shard_map/placed_0/pallas_call | solution.py:300
  62.7 6.3 %collective-permute-done.7.came_ref = bf16[12,128,128]{2,1,0:T(8,128)(2,1)S(1)} collective-permute-done((bf16[12,128,128]{2,1,0:T(8,128)(2,1)S(1)}, bf16[12,128,128]{2,1,0:T(8,128)(2,1)S(1)}, u32[]{:S(2)}, u32[]{:S(2)}) %collective-permute-start.7) | collective-permute-done | bytes 393248 | tf_op jit(solution)/shard_map/ppermute | solution.py:41
  68.9 0.9 %placed_12.1 = (bf16[24,128,128]{2,1,0:T(8,128)(2,1)}, bf16[24,128,128]{2,1,0:T(8,128)(2,1)}) custom-call(bf16[12,128,128]{2,1,0:T(8,128)(2,1)S(1)} %total_12.1.done_ref, bf16[12,128,128]{2,1,0:T(8,128)(2,1)S(1)} %collective-permute-done.7.came_ref, bf16[24,128,128]{2,1,0:T(8,128)(2,1)} %get-tuple-element.26.refs_0_, ...), custom_call_target="tpu_custom_call", output_to_operand_aliasing={{0}: (2, {}), {1}: (3, {})} | custom-call | flops 2500000000 | bytes 1048576 | tf_op jit(solution)/shard_map/placed_12/pallas_call | solution.py:300
Async XLA Ops:
  2.2 11.2 %collective-permute-start.1 = (bf16[8,128,128]{2,1,0:T(8,128)(2,1)S(1)}, bf16[8,128,128]{2,1,0:T(8,128)(2,1)S(1)}, u32[]{:S(2)}, u32[]{:S(2)}) collective-permute-start(bf16[8,128,128]{2,1,0:T(8,128)(2,1)S(1)} %get-tuple-element.23), channel_id=1, source_target_pairs={{3,0},{11,8},{19,16},{27,24},{35,32},{43,40},{51,48},{59,56},{67,6... | collective-permute-start | bytes 786440 | tf_op jit(solution)/shard_map/ppermute | solution.py:41
  3.5 16.7 %collective-permute-start = (bf16[18,128,128]{2,1,0:T(8,128)(2,1)S(1)}, bf16[18,128,128]{2,1,0:T(8,128)(2,1)S(1)}, u32[]{:S(2)}, u32[]{:S(2)}) collective-permute-start(bf16[18,128,128]{2,1,0:T(8,128)(2,1)S(1)} %get-tuple-element.22), channel_id=1, source_target_pairs={{3,4},{11,12},{19,20},{27,28},{35,36},{43,44},{51,52},{59,60},{67,... | collective-permute-start | bytes 1769480 | tf_op jit(solution)/shard_map/ppermute | solution.py:41
  5.4 14.8 %collective-permute-start.4 = (bf16[12,128,128]{2,1,0:T(8,128)(2,1)S(1)}, bf16[12,128,128]{2,1,0:T(8,128)(2,1)S(1)}, u32[]{:S(2)}, u32[]{:S(2)}) collective-permute-start(bf16[12,128,128]{2,1,0:T(8,128)(2,1)S(1)} %first.1._), channel_id=1, source_target_pairs={{0,1},{1,2},{2,3},{4,5},{5,6},{6,7},{8,9},{9,10},{10,11},{12,13},{... | collective-permute-start | bytes 1179656 | tf_op jit(solution)/shard_map/ppermute | solution.py:41
  13.3 6.9 %collective-permute-start.2 = (bf16[8,128,128]{2,1,0:T(8,128)(2,1)S(1)}, bf16[8,128,128]{2,1,0:T(8,128)(2,1)S(1)}, u32[]{:S(2)}, u32[]{:S(2)}) collective-permute-start(bf16[8,128,128]{2,1,0:T(8,128)(2,1)S(1)} %collective-permute-done.1), channel_id=1, source_target_pairs={{0,4},{8,12},{16,20},{24,28},{32,36},{40,44},{48,52},{56,60},{64,6... | collective-permute-start | bytes 786440 | tf_op jit(solution)/shard_map/ppermute | solution.py:41
  16.8 18.9 %collective-permute-start.3 = (bf16[26,128,128]{2,1,0:T(8,128)(2,1)S(1)}, bf16[26,128,128]{2,1,0:T(8,128)(2,1)S(1)}, u32[]{:S(2)}, u32[]{:S(2)}) collective-permute-start(bf16[26,128,128]{2,1,0:T(8,128)(2,1)S(1)} %get-tuple-element.24), channel_id=1, source_target_pairs={{0,1},{1,2},{2,3},{4,5},{5,6},{6,7},{8,9},{9,10},{10,11},{12,13},{... | collective-permute-start | bytes 2555912 | tf_op jit(solution)/shard_map/ppermute | solution.py:41
  20.3 22.9 %collective-permute-start.6 = (bf16[12,128,128]{2,1,0:T(8,128)(2,1)S(1)}, bf16[12,128,128]{2,1,0:T(8,128)(2,1)S(1)}, u32[]{:S(2)}, u32[]{:S(2)}) collective-permute-start(bf16[12,128,128]{2,1,0:T(8,128)(2,1)S(1)} %sent_0.1._), channel_id=1, source_target_pairs={{0,8},{1,9},{2,10},{3,11},{4,12},{5,13},{6,14},{7,15},{8,16},{9,17... | collective-permute-start | bytes 1179656 | tf_op jit(solution)/shard_map/ppermute | solution.py:41
  36.6 23.1 %collective-permute-start.5 = (bf16[12,128,128]{2,1,0:T(8,128)(2,1)S(1)}, bf16[12,128,128]{2,1,0:T(8,128)(2,1)S(1)}, u32[]{:S(2)}, u32[]{:S(2)}) collective-permute-start(bf16[12,128,128]{2,1,0:T(8,128)(2,1)S(1)} %sent_12.1._), channel_id=1, source_target_pairs={{0,8},{1,9},{2,10},{3,11},{4,12},{5,13},{6,14},{7,15},{8,16},{9,17... | collective-permute-start | bytes 1179656 | tf_op jit(solution)/shard_map/ppermute | solution.py:41
  43.3 18.5 %collective-permute-start.8 = (bf16[12,128,128]{2,1,0:T(8,128)(2,1)S(1)}, bf16[12,128,128]{2,1,0:T(8,128)(2,1)S(1)}, u32[]{:S(2)}, u32[]{:S(2)}) collective-permute-start(bf16[12,128,128]{2,1,0:T(8,128)(2,1)S(1)} %total_0.1.refs_1_.done_ref), channel_id=1, source_target_pairs={{0,64},{64,128},{128,192},{192,256},{256,320},{320,384},{384,448},... | collective-permute-start | bytes 1179656 | tf_op jit(solution)/shard_map/ppermute | solution.py:41
  59.8 9.1 %collective-permute-start.7 = (bf16[12,128,128]{2,1,0:T(8,128)(2,1)S(1)}, bf16[12,128,128]{2,1,0:T(8,128)(2,1)S(1)}, u32[]{:S(2)}, u32[]{:S(2)}) collective-permute-start(bf16[12,128,128]{2,1,0:T(8,128)(2,1)S(1)} %total_12.1.done_ref), channel_id=1, source_target_pairs={{0,64},{64,128},{128,192},{192,256},{256,320},{320,384},{384,448},... | collective-permute-start | bytes 1179656 | tf_op jit(solution)/shard_map/ppermute | solution.py:41

commit v4 on v3

--- a/solution.py
+++ b/solution.py
@@ -18,8 +18,8 @@
 PLAIN = (0, 1, 2, 4, 5, 6)
 HEAD = 18
 TAIL = CHANNELS - HEAD
-CUTS = (0, 12, 24)
-HANDED = ((0,), (1,))
+CUTS = (0, 12, 18, 24)
+HANDED = ((0,), (1,), (2,))
 CHUNKS = tuple(zip(CUTS[:-1], CUTS[1:]))
 VMEM = pl.BlockSpec(memory_space=pltpu.VMEM)
 SMEM = pl.BlockSpec(memory_space=pltpu.SMEM)

time: 70.1 us -> 68.1 us (0.971)
  the two profiles are of different devices: /device:TPU:134 before, /device:TPU:454 now
where the time goes in v4:
time: 68.1 us; the launch traced here: 67.7 us
  waiting for transfers between devices  37.2 us (55%)
  starting transfers between devices  17.2 us (25%)
  Pallas kernels  12.5 us (18%)
  between operations  0.86 us (1%)
    ppermute x11, waiting for transfers between devices, send(): return lax.ppermute(shard, axis, pairs)  37.2 us
    ppermute x11, starting transfers between devices, send(): return lax.ppermute(shard, axis, pairs)  17.2 us
    pallas_call x2, Pallas kernels, own(): pl.pallas_call(functools.partial(own_kernel, state, again), out_shape=(ar...  4.18 us
    pallas_call x4, Pallas kernels, joined(): pl.pallas_call(functools.partial(joined_kernel, state, low, high, came),...  2.96 us
    pallas_call x3, Pallas kernels, placed(): pl.pallas_call(functools.partial(placed_kernel, low, high), out_shape=(wh...  2.42 us
    pallas_call x1, Pallas kernels, loaded(): pl.pallas_call(loaded_kernel, out_shape=(array(jnp.bfloat16, CHANNELS + 2...  1.54 us
  transfers between devices with their start and end apart: 11, of which 5 were waited for; matrix products, arithmetic and copies ran while one was open for 0% of the time, Pallas kernels for 15%

profile of v4, /device:TPU:454, one launch (start us, length us, event | category | flops | bytes accessed | tf_op | source)
XLA Modules:
  0.0 67.7 jit_solution(10787789835577252473)
XLA Ops:
  0.6 1.5 %loaded.1 = (bf16[26,128,128]{2,1,0:T(8,128)(2,1)S(1)}, bf16[2,128,128]{2,1,0:T(8,128)(2,1)S(1)}, bf16[18,128,128]{2,1,0:T(8,128)(2,1)S(1)}, bf16[8,128,128]{2,1,0:T(8,128)(2,1)S(1)}, f32[4,24,24]{2,1,0:T(8,128)S(1)}) custom-call(s32[64]{0:T(128)} %sizes_hbm.1, bf16[24,128,128]{2,1,0:T(8,128)(2,1)} %bitcast.5, bf16[4,128,128]{2,1,0:T(8,128)(2,1)} %bitcast.6, ...), custom_call_target="tpu_custom_call" | custom-call | flops 2500000000 | bytes 1048576 | tf_op jit(solution)/shard_map/loaded/pallas_call | solution.py:151
  2.2 1.3 %collective-permute-start.1 = (bf16[8,128,128]{2,1,0:T(8,128)(2,1)S(1)}, bf16[8,128,128]{2,1,0:T(8,128)(2,1)S(1)}, u32[]{:S(2)}, u32[]{:S(2)}) collective-permute-start(bf16[8,128,128]{2,1,0:T(8,128)(2,1)S(1)} %get-tuple-element.25), channel_id=1, source_target_pairs={{3,0},{11,8},{19,16},{27,24},{35,32},{43,40},{51,48},{59,56},{67,6... | collective-permute-start | bytes 786440 | tf_op jit(solution)/shard_map/ppermute | solution.py:41
  3.5 0.7 %collective-permute-start = (bf16[18,128,128]{2,1,0:T(8,128)(2,1)S(1)}, bf16[18,128,128]{2,1,0:T(8,128)(2,1)S(1)}, u32[]{:S(2)}, u32[]{:S(2)}) collective-permute-start(bf16[18,128,128]{2,1,0:T(8,128)(2,1)S(1)} %get-tuple-element.24), channel_id=1, source_target_pairs={{3,4},{11,12},{19,20},{27,28},{35,36},{43,44},{51,52},{59,60},{67,... | collective-permute-start | bytes 1769480 | tf_op jit(solution)/shard_map/ppermute | solution.py:41
  4.2 1.2 %first.1._ = bf16[12,128,128]{2,1,0:T(8,128)(2,1)S(1)} custom-call(bf16[26,128,128]{2,1,0:T(8,128)(2,1)S(1)} %get-tuple-element.18.parcel_ref.cur_ref, f32[4,24,24]{2,1,0:T(8,128)S(1)} %get-tuple-element.20.weights_ref), custom_call_target="tpu_custom_call" | custom-call | flops 2500000000 | bytes 1048576 | tf_op jit(solution)/shard_map/first/pallas_call | solution.py:185
  5.4 2.9 %collective-permute-start.4 = (bf16[12,128,128]{2,1,0:T(8,128)(2,1)S(1)}, bf16[12,128,128]{2,1,0:T(8,128)(2,1)S(1)}, u32[]{:S(2)}, u32[]{:S(2)}) collective-permute-start(bf16[12,128,128]{2,1,0:T(8,128)(2,1)S(1)} %first.1._), channel_id=1, source_target_pairs={{0,1},{1,2},{2,3},{4,5},{5,6},{6,7},{8,9},{9,10},{10,11},{12,13},{... | collective-permute-start | bytes 1179656 | tf_op jit(solution)/shard_map/ppermute | solution.py:41
  8.3 5.0 %collective-permute-done.1 = bf16[8,128,128]{2,1,0:T(8,128)(2,1)S(1)} collective-permute-done((bf16[8,128,128]{2,1,0:T(8,128)(2,1)S(1)}, bf16[8,128,128]{2,1,0:T(8,128)(2,1)S(1)}, u32[]{:S(2)}, u32[]{:S(2)}) %collective-permute-start.1) | collective-permute-done | bytes 262176 | tf_op jit(solution)/shard_map/ppermute | solution.py:41
  13.3 1.3 %collective-permute-start.2 = (bf16[8,128,128]{2,1,0:T(8,128)(2,1)S(1)}, bf16[8,128,128]{2,1,0:T(8,128)(2,1)S(1)}, u32[]{:S(2)}, u32[]{:S(2)}) collective-permute-start(bf16[8,128,128]{2,1,0:T(8,128)(2,1)S(1)} %collective-permute-done.1), channel_id=1, source_target_pairs={{0,4},{8,12},{16,20},{24,28},{32,36},{40,44},{48,52},{56,60},{64,6... | collective-permute-start | bytes 786440 | tf_op jit(solution)/shard_map/ppermute | solution.py:41
  14.6 2.2 %own_2.1 = (f32[24,128,128]{2,1,0:T(8,128)S(1)}, bf16[384,768]{1,0:T(8,128)(2,1)S(1)}, bf16[26,128,128]{2,1,0:T(8,128)(2,1)S(1)}) custom-call(bf16[26,128,128]{2,1,0:T(8,128)(2,1)S(1)} %get-tuple-element.18.parcel_ref.cur_ref, bf16[2,128,128]{2,1,0:T(8,128)(2,1)S(1)} %get-tuple-element.19.even_ref, f32[4,24,24]{2,1,0:T(8,128)S(1)} %get-tuple-element.20.weights_ref, ...), custom_call_target="tpu_custom_call" | custom-call | flops 25000000 | bytes 1048576 | tf_op jit(solution)/shard_map/own_2/pallas_call | solution.py:215
  16.8 1.3 %collective-permute-start.3 = (bf16[26,128,128]{2,1,0:T(8,128)(2,1)S(1)}, bf16[26,128,128]{2,1,0:T(8,128)(2,1)S(1)}, u32[]{:S(2)}, u32[]{:S(2)}) collective-permute-start(bf16[26,128,128]{2,1,0:T(8,128)(2,1)S(1)} %get-tuple-element.26), channel_id=1, source_target_pairs={{0,1},{1,2},{2,3},{4,5},{5,6},{6,7},{8,9},{9,10},{10,11},{12,13},{... | collective-permute-start | bytes 2555912 | tf_op jit(solution)/shard_map/ppermute | solution.py:41
  18.2 2.0 %own_0.1 = (f32[24,128,128]{2,1,0:T(8,128)S(1)}, bf16[384,768]{1,0:T(8,128)(2,1)S(1)}) custom-call(bf16[26,128,128]{2,1,0:T(8,128)(2,1)S(1)} %get-tuple-element.18.parcel_ref.cur_ref, bf16[2,128,128]{2,1,0:T(8,128)(2,1)S(1)} %get-tuple-element.19.even_ref, f32[4,24,24]{2,1,0:T(8,128)S(1)} %get-tuple-element.20.weights_ref, ...), custom_call_target="tpu_custom_call" | custom-call | flops 25000000 | bytes 1048576 | tf_op jit(solution)/shard_map/own_0/pallas_call | solution.py:215
  20.2 0.0 collective-permute-done.4.plain_ref
  20.2 0.0 collective-permute-done.2.tail_ref
  20.2 0.0 collective-permute-done.head_ref
  20.2 0.1 sent_0.1._
  20.3 1.3 %collective-permute-start.7 = (bf16[12,128,128]{2,1,0:T(8,128)(2,1)S(1)}, bf16[12,128,128]{2,1,0:T(8,128)(2,1)S(1)}, u32[]{:S(2)}, u32[]{:S(2)}) collective-permute-start(bf16[12,128,128]{2,1,0:T(8,128)(2,1)S(1)} %sent_0.1._), channel_id=1, source_target_pairs={{0,8},{1,9},{2,10},{3,11},{4,12},{5,13},{6,14},{7,15},{8,16},{9,17... | collective-permute-start | bytes 1179656 | tf_op jit(solution)/shard_map/ppermute | solution.py:41
  21.6 14.1 %collective-permute-done.3.plain_ref = bf16[26,128,128]{2,1,0:T(8,128)(2,1)S(1)} collective-permute-done((bf16[26,128,128]{2,1,0:T(8,128)(2,1)S(1)}, bf16[26,128,128]{2,1,0:T(8,128)(2,1)S(1)}, u32[]{:S(2)}, u32[]{:S(2)}) %collective-permute-start.3) | collective-permute-done | bytes 852000 | tf_op jit(solution)/shard_map/ppermute | solution.py:41
  35.7 0.7 %sent_12.1._ = bf16[6,128,128]{2,1,0:T(8,128)(2,1)S(1)} custom-call(f32[24,128,128]{2,1,0:T(8,128)S(1)} %get-tuple-element.21._.base_ref, bf16[384,768]{1,0:T(8,128)(2,1)S(1)} %get-tuple-element.27.spread_ref, bf16[18,128,128]{2,1,0:T(8,128)(2,1)S(1)} %collective-permute-done.head_ref, bf16[8,128,128]{2,1,0:T(8,128)(2,1)S(1)} %collective-permute-done.2.tail_ref, ...), custom_call_target="tpu_custom_call" | custom-call | flops 2500000000 | bytes 1048576 | tf_op jit(solution)/shard_map/sent_12/pallas_call | solution.py:253
  36.4 1.3 %collective-permute-start.6 = (bf16[6,128,128]{2,1,0:T(8,128)(2,1)S(1)}, bf16[6,128,128]{2,1,0:T(8,128)(2,1)S(1)}, u32[]{:S(2)}, u32[]{:S(2)}) collective-permute-start(bf16[6,128,128]{2,1,0:T(8,128)(2,1)S(1)} %sent_12.1._), channel_id=1, source_target_pairs={{0,8},{1,9},{2,10},{3,11},{4,12},{5,13},{6,14},{7,15},{8,16},{9,17... | collective-permute-start | bytes 589832 | tf_op jit(solution)/shard_map/ppermute | solution.py:41
  37.7 0.8 %sent_18.1._ = bf16[6,128,128]{2,1,0:T(8,128)(2,1)S(1)} custom-call(f32[24,128,128]{2,1,0:T(8,128)S(1)} %get-tuple-element.21._.base_ref, bf16[384,768]{1,0:T(8,128)(2,1)S(1)} %get-tuple-element.27.spread_ref, bf16[18,128,128]{2,1,0:T(8,128)(2,1)S(1)} %collective-permute-done.head_ref, bf16[8,128,128]{2,1,0:T(8,128)(2,1)S(1)} %collective-permute-done.2.tail_ref, ...), custom_call_target="tpu_custom_call" | custom-call | flops 2500000000 | bytes 1048576 | tf_op jit(solution)/shard_map/sent_18/pallas_call | solution.py:253
  38.5 1.3 %collective-permute-start.5 = (bf16[6,128,128]{2,1,0:T(8,128)(2,1)S(1)}, bf16[6,128,128]{2,1,0:T(8,128)(2,1)S(1)}, u32[]{:S(2)}, u32[]{:S(2)}) collective-permute-start(bf16[6,128,128]{2,1,0:T(8,128)(2,1)S(1)} %sent_18.1._), channel_id=1, source_target_pairs={{0,8},{1,9},{2,10},{3,11},{4,12},{5,13},{6,14},{7,15},{8,16},{9,17... | collective-permute-start | bytes 589832 | tf_op jit(solution)/shard_map/ppermute | solution.py:41
  39.8 1.4 %kept.1.kept_ref.refs_1_ = f32[24,128,128]{2,1,0:T(8,128)S(1)} custom-call(f32[24,128,128]{2,1,0:T(8,128)S(1)} %get-tuple-element.22._.base_ref, bf16[384,768]{1,0:T(8,128)(2,1)S(1)} %get-tuple-element.23.spread_ref, bf16[18,128,128]{2,1,0:T(8,128)(2,1)S(1)} %collective-permute-done.head_ref, bf16[8,128,128]{2,1,0:T(8,128)(2,1)S(1)} %collective-permute-done.2.tail_ref, ...), custom_call_target="tpu_custom_call" | custom-call | flops 2500000000 | bytes 1048576 | tf_op jit(solution)/shard_map/kept/pallas_call | solution.py:253
  41.2 0.0 collective-permute-done.7.refs_0_
  41.2 0.1 total_0.1.refs_1_.done_ref
  41.3 1.9 %collective-permute-start.10 = (bf16[12,128,128]{2,1,0:T(8,128)(2,1)S(1)}, bf16[12,128,128]{2,1,0:T(8,128)(2,1)S(1)}, u32[]{:S(2)}, u32[]{:S(2)}) collective-permute-start(bf16[12,128,128]{2,1,0:T(8,128)(2,1)S(1)} %total_0.1.refs_1_.done_ref), channel_id=1, source_target_pairs={{0,64},{64,128},{128,192},{192,256},{256,320},{320,384},{384,448},... | collective-permute-start | bytes 1179656 | tf_op jit(solution)/shard_map/ppermute | solution.py:41
  43.2 6.6 %collective-permute-done.6.refs_0_ = bf16[6,128,128]{2,1,0:T(8,128)(2,1)S(1)} collective-permute-done((bf16[6,128,128]{2,1,0:T(8,128)(2,1)S(1)}, bf16[6,128,128]{2,1,0:T(8,128)(2,1)S(1)}, u32[]{:S(2)}, u32[]{:S(2)}) %collective-permute-start.6) | collective-permute-done | bytes 196640 | tf_op jit(solution)/shard_map/ppermute | solution.py:41
  49.9 1.9 %collective-permute-start.9 = (bf16[6,128,128]{2,1,0:T(8,128)(2,1)S(1)}, bf16[6,128,128]{2,1,0:T(8,128)(2,1)S(1)}, u32[]{:S(2)}, u32[]{:S(2)}) collective-permute-start(bf16[6,128,128]{2,1,0:T(8,128)(2,1)S(1)} %total_12.1.refs_1_.done_ref), channel_id=1, source_target_pairs={{0,64},{64,128},{128,192},{192,256},{256,320},{320,384},{384,448},... | collective-permute-start | bytes 589832 | tf_op jit(solution)/shard_map/ppermute | solution.py:41
  51.8 8.1 %collective-permute-done.5.refs_0_ = bf16[6,128,128]{2,1,0:T(8,128)(2,1)S(1)} collective-permute-done((bf16[6,128,128]{2,1,0:T(8,128)(2,1)S(1)}, bf16[6,128,128]{2,1,0:T(8,128)(2,1)S(1)}, u32[]{:S(2)}, u32[]{:S(2)}) %collective-permute-start.5) | collective-permute-done | bytes 196640 | tf_op jit(solution)/shard_map/ppermute | solution.py:41
  60.0 1.9 %collective-permute-start.8 = (bf16[6,128,128]{2,1,0:T(8,128)(2,1)S(1)}, bf16[6,128,128]{2,1,0:T(8,128)(2,1)S(1)}, u32[]{:S(2)}, u32[]{:S(2)}) collective-permute-start(bf16[6,128,128]{2,1,0:T(8,128)(2,1)S(1)} %total_18.1.done_ref), channel_id=1, source_target_pairs={{0,64},{64,128},{128,192},{192,256},{256,320},{320,384},{384,448},... | collective-permute-start | bytes 589832 | tf_op jit(solution)/shard_map/ppermute | solution.py:41
  61.9 0.0 collective-permute-done.10.came_ref
  61.9 0.9 %placed_0.1 = (bf16[24,128,128]{2,1,0:T(8,128)(2,1)}, bf16[24,128,128]{2,1,0:T(8,128)(2,1)}) custom-call(bf16[12,128,128]{2,1,0:T(8,128)(2,1)S(1)} %total_0.1.refs_1_.done_ref, bf16[12,128,128]{2,1,0:T(8,128)(2,1)S(1)} %collective-permute-done.10.came_ref), custom_call_target="tpu_custom_call" | custom-call | flops 24999999488 | bytes 1048576 | tf_op jit(solution)/shard_map/placed_0/pallas_call | solution.py:300
  62.8 0.0 collective-permute-done.9.came_ref
  62.8 0.8 %placed_12.1 = (bf16[24,128,128]{2,1,0:T(8,128)(2,1)}, bf16[24,128,128]{2,1,0:T(8,128)(2,1)}) custom-call(bf16[6,128,128]{2,1,0:T(8,128)(2,1)S(1)} %total_12.1.refs_1_.done_ref, bf16[6,128,128]{2,1,0:T(8,128)(2,1)S(1)} %collective-permute-done.9.came_ref, ...), custom_call_target="tpu_custom_call", output_to_operand_aliasing={{0}: (2, {}), {1}: (3, {})} | custom-call | flops 24999999488 | bytes 1048576 | tf_op jit(solution)/shard_map/placed_12/pallas_call | solution.py:300
  63.6 3.4 %collective-permute-done.8.came_ref = bf16[6,128,128]{2,1,0:T(8,128)(2,1)S(1)} collective-permute-done((bf16[6,128,128]{2,1,0:T(8,128)(2,1)S(1)}, bf16[6,128,128]{2,1,0:T(8,128)(2,1)S(1)}, u32[]{:S(2)}, u32[]{:S(2)}) %collective-permute-start.8) | collective-permute-done | bytes 196640 | tf_op jit(solution)/shard_map/ppermute | solution.py:41
  67.0 0.8 %placed_18.1 = (bf16[24,128,128]{2,1,0:T(8,128)(2,1)}, bf16[24,128,128]{2,1,0:T(8,128)(2,1)}) custom-call(bf16[6,128,128]{2,1,0:T(8,128)(2,1)S(1)} %total_18.1.done_ref, bf16[6,128,128]{2,1,0:T(8,128)(2,1)S(1)} %collective-permute-done.8.came_ref, bf16[24,128,128]{2,1,0:T(8,128)(2,1)} %get-tuple-element.30.refs_0_, ...), custom_call_target="tpu_custom_call", output_to_operand_aliasing={{0}: (2, {}), {1}: (3, {})} | custom-call | flops 2500000000 | bytes 1048576 | tf_op jit(solution)/shard_map/placed_18/pallas_call | solution.py:300
  (2 shorter events, 0.1 us)
Async XLA Ops:
  2.2 11.2 %collective-permute-start.1 = (bf16[8,128,128]{2,1,0:T(8,128)(2,1)S(1)}, bf16[8,128,128]{2,1,0:T(8,128)(2,1)S(1)}, u32[]{:S(2)}, u32[]{:S(2)}) collective-permute-start(bf16[8,128,128]{2,1,0:T(8,128)(2,1)S(1)} %get-tuple-element.25), channel_id=1, source_target_pairs={{3,0},{11,8},{19,16},{27,24},{35,32},{43,40},{51,48},{59,56},{67,6... | collective-permute-start | bytes 786440 | tf_op jit(solution)/shard_map/ppermute | solution.py:41
  3.5 16.7 %collective-permute-start = (bf16[18,128,128]{2,1,0:T(8,128)(2,1)S(1)}, bf16[18,128,128]{2,1,0:T(8,128)(2,1)S(1)}, u32[]{:S(2)}, u32[]{:S(2)}) collective-permute-start(bf16[18,128,128]{2,1,0:T(8,128)(2,1)S(1)} %get-tuple-element.24), channel_id=1, source_target_pairs={{3,4},{11,12},{19,20},{27,28},{35,36},{43,44},{51,52},{59,60},{67,... | collective-permute-start | bytes 1769480 | tf_op jit(solution)/shard_map/ppermute | solution.py:41
  5.4 14.8 %collective-permute-start.4 = (bf16[12,128,128]{2,1,0:T(8,128)(2,1)S(1)}, bf16[12,128,128]{2,1,0:T(8,128)(2,1)S(1)}, u32[]{:S(2)}, u32[]{:S(2)}) collective-permute-start(bf16[12,128,128]{2,1,0:T(8,128)(2,1)S(1)} %first.1._), channel_id=1, source_target_pairs={{0,1},{1,2},{2,3},{4,5},{5,6},{6,7},{8,9},{9,10},{10,11},{12,13},{... | collective-permute-start | bytes 1179656 | tf_op jit(solution)/shard_map/ppermute | solution.py:41
  13.3 6.9 %collective-permute-start.2 = (bf16[8,128,128]{2,1,0:T(8,128)(2,1)S(1)}, bf16[8,128,128]{2,1,0:T(8,128)(2,1)S(1)}, u32[]{:S(2)}, u32[]{:S(2)}) collective-permute-start(bf16[8,128,128]{2,1,0:T(8,128)(2,1)S(1)} %collective-permute-done.1), channel_id=1, source_target_pairs={{0,4},{8,12},{16,20},{24,28},{32,36},{40,44},{48,52},{56,60},{64,6... | collective-permute-start | bytes 786440 | tf_op jit(solution)/shard_map/ppermute | solution.py:41
  16.8 18.9 %collective-permute-start.3 = (bf16[26,128,128]{2,1,0:T(8,128)(2,1)S(1)}, bf16[26,128,128]{2,1,0:T(8,128)(2,1)S(1)}, u32[]{:S(2)}, u32[]{:S(2)}) collective-permute-start(bf16[26,128,128]{2,1,0:T(8,128)(2,1)S(1)} %get-tuple-element.26), channel_id=1, source_target_pairs={{0,1},{1,2},{2,3},{4,5},{5,6},{6,7},{8,9},{9,10},{10,11},{12,13},{... | collective-permute-start | bytes 2555912 | tf_op jit(solution)/shard_map/ppermute | solution.py:41
  20.3 20.9 %collective-permute-start.7 = (bf16[12,128,128]{2,1,0:T(8,128)(2,1)S(1)}, bf16[12,128,128]{2,1,0:T(8,128)(2,1)S(1)}, u32[]{:S(2)}, u32[]{:S(2)}) collective-permute-start(bf16[12,128,128]{2,1,0:T(8,128)(2,1)S(1)} %sent_0.1._), channel_id=1, source_target_pairs={{0,8},{1,9},{2,10},{3,11},{4,12},{5,13},{6,14},{7,15},{8,16},{9,17... | collective-permute-start | bytes 1179656 | tf_op jit(solution)/shard_map/ppermute | solution.py:41
  36.4 13.4 %collective-permute-start.6 = (bf16[6,128,128]{2,1,0:T(8,128)(2,1)S(1)}, bf16[6,128,128]{2,1,0:T(8,128)(2,1)S(1)}, u32[]{:S(2)}, u32[]{:S(2)}) collective-permute-start(bf16[6,128,128]{2,1,0:T(8,128)(2,1)S(1)} %sent_12.1._), channel_id=1, source_target_pairs={{0,8},{1,9},{2,10},{3,11},{4,12},{5,13},{6,14},{7,15},{8,16},{9,17... | collective-permute-start | bytes 589832 | tf_op jit(solution)/shard_map/ppermute | solution.py:41
  38.5 21.4 %collective-permute-start.5 = (bf16[6,128,128]{2,1,0:T(8,128)(2,1)S(1)}, bf16[6,128,128]{2,1,0:T(8,128)(2,1)S(1)}, u32[]{:S(2)}, u32[]{:S(2)}) collective-permute-start(bf16[6,128,128]{2,1,0:T(8,128)(2,1)S(1)} %sent_18.1._), channel_id=1, source_target_pairs={{0,8},{1,9},{2,10},{3,11},{4,12},{5,13},{6,14},{7,15},{8,16},{9,17... | collective-permute-start | bytes 589832 | tf_op jit(solution)/shard_map/ppermute | solution.py:41
  41.3 20.6 %collective-permute-start.10 = (bf16[12,128,128]{2,1,0:T(8,128)(2,1)S(1)}, bf16[12,128,128]{2,1,0:T(8,128)(2,1)S(1)}, u32[]{:S(2)}, u32[]{:S(2)}) collective-permute-start(bf16[12,128,128]{2,1,0:T(8,128)(2,1)S(1)} %total_0.1.refs_1_.done_ref), channel_id=1, source_target_pairs={{0,64},{64,128},{128,192},{192,256},{256,320},{320,384},{384,448},... | collective-permute-start | bytes 1179656 | tf_op jit(solution)/shard_map/ppermute | solution.py:41
  49.9 12.9 %collective-permute-start.9 = (bf16[6,128,128]{2,1,0:T(8,128)(2,1)S(1)}, bf16[6,128,128]{2,1,0:T(8,128)(2,1)S(1)}, u32[]{:S(2)}, u32[]{:S(2)}) collective-permute-start(bf16[6,128,128]{2,1,0:T(8,128)(2,1)S(1)} %total_12.1.refs_1_.done_ref), channel_id=1, source_target_pairs={{0,64},{64,128},{128,192},{192,256},{256,320},{320,384},{384,448},... | collective-permute-start | bytes 589832 | tf_op jit(solution)/shard_map/ppermute | solution.py:41
  60.0 7.0 %collective-permute-start.8 = (bf16[6,128,128]{2,1,0:T(8,128)(2,1)S(1)}, bf16[6,128,128]{2,1,0:T(8,128)(2,1)S(1)}, u32[]{:S(2)}, u32[]{:S(2)}) collective-permute-start(bf16[6,128,128]{2,1,0:T(8,128)(2,1)S(1)} %total_18.1.done_ref), channel_id=1, source_target_pairs={{0,64},{64,128},{128,192},{192,256},{256,320},{320,384},{384,448},... | collective-permute-start | bytes 589832 | tf_op jit(solution)/shard_map/ppermute | solution.py:41

commit v5 on v4

--- a/solution.py
+++ b/solution.py
@@ -16,7 +16,7 @@
 ROWS = CHANNELS * TILE
 CARRY = 3
 PLAIN = (0, 1, 2, 4, 5, 6)
-HEAD = 18
+HEAD = 16
 TAIL = CHANNELS - HEAD
 CUTS = (0, 12, 18, 24)
 HANDED = ((0,), (1,), (2,))

time: 68.1 us -> 69.6 us (1.022)
  waiting for transfers between devices: 37.2 us -> 38.7 us
    ppermute x11, waiting for transfers between devices: 37.2 us -> 38.7 us  [send(): return lax.ppermute(shard, axis, pairs)]
  transfers between devices with their start and end apart: 11 -> 11, of which waited for: 5 -> 6; matrix products, arithmetic and copies ran while one was open for 0% -> 0% of each run, Pallas kernels for 15% -> 15%
where the time goes in v5:
time: 69.6 us; the launch traced here: 69.2 us
  waiting for transfers between devices  38.7 us (56%)
  starting transfers between devices  17.2 us (25%)
  Pallas kernels  12.4 us (18%)
  between operations  0.85 us (1%)
    ppermute x11, waiting for transfers between devices, send(): return lax.ppermute(shard, axis, pairs)  38.7 us
    ppermute x11, starting transfers between devices, send(): return lax.ppermute(shard, axis, pairs)  17.2 us
    pallas_call x2, Pallas kernels, own(): pl.pallas_call(functools.partial(own_kernel, state, again), out_shape=(ar...  4.19 us
    pallas_call x4, Pallas kernels, joined(): pl.pallas_call(functools.partial(joined_kernel, state, low, high, came),...  2.94 us
    pallas_call x3, Pallas kernels, placed(): pl.pallas_call(functools.partial(placed_kernel, low, high), out_shape=(wh...  2.42 us
    pallas_call x1, Pallas kernels, loaded(): pl.pallas_call(loaded_kernel, out_shape=(array(jnp.bfloat16, CHANNELS + 2...  1.53 us
  transfers between devices with their start and end apart: 11, of which 6 were waited for; matrix products, arithmetic and copies ran while one was open for 0% of the time, Pallas kernels for 15%

profile of v5, /device:TPU:454, one launch (start us, length us, event | category | flops | bytes accessed | tf_op | source)
XLA Modules:
  0.0 69.2 jit_solution(4775578444815466445)
XLA Ops:
  0.6 1.5 %loaded.1 = (bf16[26,128,128]{2,1,0:T(8,128)(2,1)S(1)}, bf16[2,128,128]{2,1,0:T(8,128)(2,1)S(1)}, bf16[16,128,128]{2,1,0:T(8,128)(2,1)S(1)}, bf16[10,128,128]{2,1,0:T(8,128)(2,1)S(1)}, f32[4,24,24]{2,1,0:T(8,128)S(1)}) custom-call(s32[64]{0:T(128)} %sizes_hbm.1, bf16[24,128,128]{2,1,0:T(8,128)(2,1)} %bitcast.5, bf16[4,128,128]{2,1,0:T(8,128)(2,1)} %bitcast.6, ...), custom_call_target="tpu_custom_call" | custom-call | flops 2500000000 | bytes 1048576 | tf_op jit(solution)/shard_map/loaded/pallas_call | solution.py:151
  2.2 1.3 %collective-permute-start.1 = (bf16[10,128,128]{2,1,0:T(8,128)(2,1)S(1)}, bf16[10,128,128]{2,1,0:T(8,128)(2,1)S(1)}, u32[]{:S(2)}, u32[]{:S(2)}) collective-permute-start(bf16[10,128,128]{2,1,0:T(8,128)(2,1)S(1)} %get-tuple-element.25), channel_id=1, source_target_pairs={{3,0},{11,8},{19,16},{27,24},{35,32},{43,40},{51,48},{59,56},{67,6... | collective-permute-start | bytes 983048 | tf_op jit(solution)/shard_map/ppermute | solution.py:41
  3.5 0.7 %collective-permute-start = (bf16[16,128,128]{2,1,0:T(8,128)(2,1)S(1)}, bf16[16,128,128]{2,1,0:T(8,128)(2,1)S(1)}, u32[]{:S(2)}, u32[]{:S(2)}) collective-permute-start(bf16[16,128,128]{2,1,0:T(8,128)(2,1)S(1)} %get-tuple-element.24), channel_id=1, source_target_pairs={{3,4},{11,12},{19,20},{27,28},{35,36},{43,44},{51,52},{59,60},{67,... | collective-permute-start | bytes 1572872 | tf_op jit(solution)/shard_map/ppermute | solution.py:41
  4.2 1.2 %first.1._ = bf16[12,128,128]{2,1,0:T(8,128)(2,1)S(1)} custom-call(bf16[26,128,128]{2,1,0:T(8,128)(2,1)S(1)} %get-tuple-element.18.parcel_ref.cur_ref, f32[4,24,24]{2,1,0:T(8,128)S(1)} %get-tuple-element.20.weights_ref), custom_call_target="tpu_custom_call" | custom-call | flops 2500000000 | bytes 1048576 | tf_op jit(solution)/shard_map/first/pallas_call | solution.py:185
  5.4 2.9 %collective-permute-start.4 = (bf16[12,128,128]{2,1,0:T(8,128)(2,1)S(1)}, bf16[12,128,128]{2,1,0:T(8,128)(2,1)S(1)}, u32[]{:S(2)}, u32[]{:S(2)}) collective-permute-start(bf16[12,128,128]{2,1,0:T(8,128)(2,1)S(1)} %first.1._), channel_id=1, source_target_pairs={{0,1},{1,2},{2,3},{4,5},{5,6},{6,7},{8,9},{9,10},{10,11},{12,13},{... | collective-permute-start | bytes 1179656 | tf_op jit(solution)/shard_map/ppermute | solution.py:41
  8.3 6.4 %collective-permute-done.1 = bf16[10,128,128]{2,1,0:T(8,128)(2,1)S(1)} collective-permute-done((bf16[10,128,128]{2,1,0:T(8,128)(2,1)S(1)}, bf16[10,128,128]{2,1,0:T(8,128)(2,1)S(1)}, u32[]{:S(2)}, u32[]{:S(2)}) %collective-permute-start.1) | collective-permute-done | bytes 327712 | tf_op jit(solution)/shard_map/ppermute | solution.py:41
  14.7 1.3 %collective-permute-start.2 = (bf16[10,128,128]{2,1,0:T(8,128)(2,1)S(1)}, bf16[10,128,128]{2,1,0:T(8,128)(2,1)S(1)}, u32[]{:S(2)}, u32[]{:S(2)}) collective-permute-start(bf16[10,128,128]{2,1,0:T(8,128)(2,1)S(1)} %collective-permute-done.1), channel_id=1, source_target_pairs={{0,4},{8,12},{16,20},{24,28},{32,36},{40,44},{48,52},{56,60},{64,6... | collective-permute-start | bytes 983048 | tf_op jit(solution)/shard_map/ppermute | solution.py:41
  16.0 2.2 %own_2.1 = (f32[24,128,128]{2,1,0:T(8,128)S(1)}, bf16[384,768]{1,0:T(8,128)(2,1)S(1)}, bf16[26,128,128]{2,1,0:T(8,128)(2,1)S(1)}) custom-call(bf16[26,128,128]{2,1,0:T(8,128)(2,1)S(1)} %get-tuple-element.18.parcel_ref.cur_ref, bf16[2,128,128]{2,1,0:T(8,128)(2,1)S(1)} %get-tuple-element.19.even_ref, f32[4,24,24]{2,1,0:T(8,128)S(1)} %get-tuple-element.20.weights_ref, ...), custom_call_target="tpu_custom_call" | custom-call | flops 25000000 | bytes 1048576 | tf_op jit(solution)/shard_map/own_2/pallas_call | solution.py:215
  18.2 1.3 %collective-permute-start.3 = (bf16[26,128,128]{2,1,0:T(8,128)(2,1)S(1)}, bf16[26,128,128]{2,1,0:T(8,128)(2,1)S(1)}, u32[]{:S(2)}, u32[]{:S(2)}) collective-permute-start(bf16[26,128,128]{2,1,0:T(8,128)(2,1)S(1)} %get-tuple-element.26), channel_id=1, source_target_pairs={{0,1},{1,2},{2,3},{4,5},{5,6},{6,7},{8,9},{9,10},{10,11},{12,13},{... | collective-permute-start | bytes 2555912 | tf_op jit(solution)/shard_map/ppermute | solution.py:41
  19.6 2.0 %own_0.1 = (f32[24,128,128]{2,1,0:T(8,128)S(1)}, bf16[384,768]{1,0:T(8,128)(2,1)S(1)}) custom-call(bf16[26,128,128]{2,1,0:T(8,128)(2,1)S(1)} %get-tuple-element.18.parcel_ref.cur_ref, bf16[2,128,128]{2,1,0:T(8,128)(2,1)S(1)} %get-tuple-element.19.even_ref, f32[4,24,24]{2,1,0:T(8,128)S(1)} %get-tuple-element.20.weights_ref, ...), custom_call_target="tpu_custom_call" | custom-call | flops 25000000 | bytes 1048576 | tf_op jit(solution)/shard_map/own_0/pallas_call | solution.py:215
  21.6 0.0 collective-permute-done.4.plain_ref
  21.6 0.0 collective-permute-done.head_ref
  21.6 0.8 %collective-permute-done.2.tail_ref = bf16[10,128,128]{2,1,0:T(8,128)(2,1)S(1)} collective-permute-done((bf16[10,128,128]{2,1,0:T(8,128)(2,1)S(1)}, bf16[10,128,128]{2,1,0:T(8,128)(2,1)S(1)}, u32[]{:S(2)}, u32[]{:S(2)}) %collective-permute-start.2) | collective-permute-done | bytes 327712 | tf_op jit(solution)/shard_map/ppermute | solution.py:41
  22.4 0.1 sent_0.1._
  22.4 1.3 %collective-permute-start.7 = (bf16[12,128,128]{2,1,0:T(8,128)(2,1)S(1)}, bf16[12,128,128]{2,1,0:T(8,128)(2,1)S(1)}, u32[]{:S(2)}, u32[]{:S(2)}) collective-permute-start(bf16[12,128,128]{2,1,0:T(8,128)(2,1)S(1)} %sent_0.1._), channel_id=1, source_target_pairs={{0,8},{1,9},{2,10},{3,11},{4,12},{5,13},{6,14},{7,15},{8,16},{9,17... | collective-permute-start | bytes 1179656 | tf_op jit(solution)/shard_map/ppermute | solution.py:41
  23.7 13.3 %collective-permute-done.3.plain_ref = bf16[26,128,128]{2,1,0:T(8,128)(2,1)S(1)} collective-permute-done((bf16[26,128,128]{2,1,0:T(8,128)(2,1)S(1)}, bf16[26,128,128]{2,1,0:T(8,128)(2,1)S(1)}, u32[]{:S(2)}, u32[]{:S(2)}) %collective-permute-start.3) | collective-permute-done | bytes 852000 | tf_op jit(solution)/shard_map/ppermute | solution.py:41
  37.1 0.7 %sent_12.1._ = bf16[6,128,128]{2,1,0:T(8,128)(2,1)S(1)} custom-call(f32[24,128,128]{2,1,0:T(8,128)S(1)} %get-tuple-element.21._.base_ref, bf16[384,768]{1,0:T(8,128)(2,1)S(1)} %get-tuple-element.27.spread_ref, bf16[16,128,128]{2,1,0:T(8,128)(2,1)S(1)} %collective-permute-done.head_ref, bf16[10,128,128]{2,1,0:T(8,128)(2,1)S(1)} %collective-permute-done.2.tail_ref, ...), custom_call_target="tpu_custom_call" | custom-call | flops 2500000000 | bytes 1048576 | tf_op jit(solution)/shard_map/sent_12/pallas_call | solution.py:253
  37.8 1.3 %collective-permute-start.6 = (bf16[6,128,128]{2,1,0:T(8,128)(2,1)S(1)}, bf16[6,128,128]{2,1,0:T(8,128)(2,1)S(1)}, u32[]{:S(2)}, u32[]{:S(2)}) collective-permute-start(bf16[6,128,128]{2,1,0:T(8,128)(2,1)S(1)} %sent_12.1._), channel_id=1, source_target_pairs={{0,8},{1,9},{2,10},{3,11},{4,12},{5,13},{6,14},{7,15},{8,16},{9,17... | collective-permute-start | bytes 589832 | tf_op jit(solution)/shard_map/ppermute | solution.py:41
  39.1 0.8 %sent_18.1._ = bf16[6,128,128]{2,1,0:T(8,128)(2,1)S(1)} custom-call(f32[24,128,128]{2,1,0:T(8,128)S(1)} %get-tuple-element.21._.base_ref, bf16[384,768]{1,0:T(8,128)(2,1)S(1)} %get-tuple-element.27.spread_ref, bf16[16,128,128]{2,1,0:T(8,128)(2,1)S(1)} %collective-permute-done.head_ref, bf16[10,128,128]{2,1,0:T(8,128)(2,1)S(1)} %collective-permute-done.2.tail_ref, ...), custom_call_target="tpu_custom_call" | custom-call | flops 2500000000 | bytes 1048576 | tf_op jit(solution)/shard_map/sent_18/pallas_call | solution.py:253
  39.9 1.3 %collective-permute-start.5 = (bf16[6,128,128]{2,1,0:T(8,128)(2,1)S(1)}, bf16[6,128,128]{2,1,0:T(8,128)(2,1)S(1)}, u32[]{:S(2)}, u32[]{:S(2)}) collective-permute-start(bf16[6,128,128]{2,1,0:T(8,128)(2,1)S(1)} %sent_18.1._), channel_id=1, source_target_pairs={{0,8},{1,9},{2,10},{3,11},{4,12},{5,13},{6,14},{7,15},{8,16},{9,17... | collective-permute-start | bytes 589832 | tf_op jit(solution)/shard_map/ppermute | solution.py:41
  41.2 1.4 %kept.1.kept_ref.refs_1_ = f32[24,128,128]{2,1,0:T(8,128)S(1)} custom-call(f32[24,128,128]{2,1,0:T(8,128)S(1)} %get-tuple-element.22._.base_ref, bf16[384,768]{1,0:T(8,128)(2,1)S(1)} %get-tuple-element.23.spread_ref, bf16[16,128,128]{2,1,0:T(8,128)(2,1)S(1)} %collective-permute-done.head_ref, bf16[10,128,128]{2,1,0:T(8,128)(2,1)S(1)} %collective-permute-done.2.tail_ref, ...), custom_call_target="tpu_custom_call" | custom-call | flops 2500000000 | bytes 1048576 | tf_op jit(solution)/shard_map/kept/pallas_call | solution.py:253
  42.6 0.0 collective-permute-done.7.refs_0_
  42.6 0.1 total_0.1.refs_1_.done_ref
  42.7 1.9 %collective-permute-start.10 = (bf16[12,128,128]{2,1,0:T(8,128)(2,1)S(1)}, bf16[12,128,128]{2,1,0:T(8,128)(2,1)S(1)}, u32[]{:S(2)}, u32[]{:S(2)}) collective-permute-start(bf16[12,128,128]{2,1,0:T(8,128)(2,1)S(1)} %total_0.1.refs_1_.done_ref), channel_id=1, source_target_pairs={{0,64},{64,128},{128,192},{192,256},{256,320},{320,384},{384,448},... | collective-permute-start | bytes 1179656 | tf_op jit(solution)/shard_map/ppermute | solution.py:41
  44.6 6.5 %collective-permute-done.6.refs_0_ = bf16[6,128,128]{2,1,0:T(8,128)(2,1)S(1)} collective-permute-done((bf16[6,128,128]{2,1,0:T(8,128)(2,1)S(1)}, bf16[6,128,128]{2,1,0:T(8,128)(2,1)S(1)}, u32[]{:S(2)}, u32[]{:S(2)}) %collective-permute-start.6) | collective-permute-done | bytes 196640 | tf_op jit(solution)/shard_map/ppermute | solution.py:41
  51.1 1.9 %collective-permute-start.9 = (bf16[6,128,128]{2,1,0:T(8,128)(2,1)S(1)}, bf16[6,128,128]{2,1,0:T(8,128)(2,1)S(1)}, u32[]{:S(2)}, u32[]{:S(2)}) collective-permute-start(bf16[6,128,128]{2,1,0:T(8,128)(2,1)S(1)} %total_12.1.refs_1_.done_ref), channel_id=1, source_target_pairs={{0,64},{64,128},{128,192},{192,256},{256,320},{320,384},{384,448},... | collective-permute-start | bytes 589832 | tf_op jit(solution)/shard_map/ppermute | solution.py:41
  53.1 8.3 %collective-permute-done.5.refs_0_ = bf16[6,128,128]{2,1,0:T(8,128)(2,1)S(1)} collective-permute-done((bf16[6,128,128]{2,1,0:T(8,128)(2,1)S(1)}, bf16[6,128,128]{2,1,0:T(8,128)(2,1)S(1)}, u32[]{:S(2)}, u32[]{:S(2)}) %collective-permute-start.5) | collective-permute-done | bytes 196640 | tf_op jit(solution)/shard_map/ppermute | solution.py:41
  61.5 1.9 %collective-permute-start.8 = (bf16[6,128,128]{2,1,0:T(8,128)(2,1)S(1)}, bf16[6,128,128]{2,1,0:T(8,128)(2,1)S(1)}, u32[]{:S(2)}, u32[]{:S(2)}) collective-permute-start(bf16[6,128,128]{2,1,0:T(8,128)(2,1)S(1)} %total_18.1.done_ref), channel_id=1, source_target_pairs={{0,64},{64,128},{128,192},{192,256},{256,320},{320,384},{384,448},... | collective-permute-start | bytes 589832 | tf_op jit(solution)/shard_map/ppermute | solution.py:41
  63.4 0.0 collective-permute-done.10.came_ref
  63.4 0.9 %placed_0.1 = (bf16[24,128,128]{2,1,0:T(8,128)(2,1)}, bf16[24,128,128]{2,1,0:T(8,128)(2,1)}) custom-call(bf16[12,128,128]{2,1,0:T(8,128)(2,1)S(1)} %total_0.1.refs_1_.done_ref, bf16[12,128,128]{2,1,0:T(8,128)(2,1)S(1)} %collective-permute-done.10.came_ref), custom_call_target="tpu_custom_call" | custom-call | flops 24999999488 | bytes 1048576 | tf_op jit(solution)/shard_map/placed_0/pallas_call | solution.py:300
  64.3 0.0 collective-permute-done.9.came_ref
  64.3 0.8 %placed_12.1 = (bf16[24,128,128]{2,1,0:T(8,128)(2,1)}, bf16[24,128,128]{2,1,0:T(8,128)(2,1)}) custom-call(bf16[6,128,128]{2,1,0:T(8,128)(2,1)S(1)} %total_12.1.refs_1_.done_ref, bf16[6,128,128]{2,1,0:T(8,128)(2,1)S(1)} %collective-permute-done.9.came_ref, ...), custom_call_target="tpu_custom_call", output_to_operand_aliasing={{0}: (2, {}), {1}: (3, {})} | custom-call | flops 24999999488 | bytes 1048576 | tf_op jit(solution)/shard_map/placed_12/pallas_call | solution.py:300
  65.1 3.4 %collective-permute-done.8.came_ref = bf16[6,128,128]{2,1,0:T(8,128)(2,1)S(1)} collective-permute-done((bf16[6,128,128]{2,1,0:T(8,128)(2,1)S(1)}, bf16[6,128,128]{2,1,0:T(8,128)(2,1)S(1)}, u32[]{:S(2)}, u32[]{:S(2)}) %collective-permute-start.8) | collective-permute-done | bytes 196640 | tf_op jit(solution)/shard_map/ppermute | solution.py:41
  68.4 0.8 %placed_18.1 = (bf16[24,128,128]{2,1,0:T(8,128)(2,1)}, bf16[24,128,128]{2,1,0:T(8,128)(2,1)}) custom-call(bf16[6,128,128]{2,1,0:T(8,128)(2,1)S(1)} %total_18.1.done_ref, bf16[6,128,128]{2,1,0:T(8,128)(2,1)S(1)} %collective-permute-done.8.came_ref, bf16[24,128,128]{2,1,0:T(8,128)(2,1)} %get-tuple-element.30.refs_0_, ...), custom_call_target="tpu_custom_call", output_to_operand_aliasing={{0}: (2, {}), {1}: (3, {})} | custom-call | flops 2500000000 | bytes 1048576 | tf_op jit(solution)/shard_map/placed_18/pallas_call | solution.py:300
  (2 shorter events, 0.1 us)
Async XLA Ops:
  2.2 12.6 %collective-permute-start.1 = (bf16[10,128,128]{2,1,0:T(8,128)(2,1)S(1)}, bf16[10,128,128]{2,1,0:T(8,128)(2,1)S(1)}, u32[]{:S(2)}, u32[]{:S(2)}) collective-permute-start(bf16[10,128,128]{2,1,0:T(8,128)(2,1)S(1)} %get-tuple-element.25), channel_id=1, source_target_pairs={{3,0},{11,8},{19,16},{27,24},{35,32},{43,40},{51,48},{59,56},{67,6... | collective-permute-start | bytes 983048 | tf_op jit(solution)/shard_map/ppermute | solution.py:41
  3.5 18.1 %collective-permute-start = (bf16[16,128,128]{2,1,0:T(8,128)(2,1)S(1)}, bf16[16,128,128]{2,1,0:T(8,128)(2,1)S(1)}, u32[]{:S(2)}, u32[]{:S(2)}) collective-permute-start(bf16[16,128,128]{2,1,0:T(8,128)(2,1)S(1)} %get-tuple-element.24), channel_id=1, source_target_pairs={{3,4},{11,12},{19,20},{27,28},{35,36},{43,44},{51,52},{59,60},{67,... | collective-permute-start | bytes 1572872 | tf_op jit(solution)/shard_map/ppermute | solution.py:41
  5.4 16.2 %collective-permute-start.4 = (bf16[12,128,128]{2,1,0:T(8,128)(2,1)S(1)}, bf16[12,128,128]{2,1,0:T(8,128)(2,1)S(1)}, u32[]{:S(2)}, u32[]{:S(2)}) collective-permute-start(bf16[12,128,128]{2,1,0:T(8,128)(2,1)S(1)} %first.1._), channel_id=1, source_target_pairs={{0,1},{1,2},{2,3},{4,5},{5,6},{6,7},{8,9},{9,10},{10,11},{12,13},{... | collective-permute-start | bytes 1179656 | tf_op jit(solution)/shard_map/ppermute | solution.py:41
  14.7 7.6 %collective-permute-start.2 = (bf16[10,128,128]{2,1,0:T(8,128)(2,1)S(1)}, bf16[10,128,128]{2,1,0:T(8,128)(2,1)S(1)}, u32[]{:S(2)}, u32[]{:S(2)}) collective-permute-start(bf16[10,128,128]{2,1,0:T(8,128)(2,1)S(1)} %collective-permute-done.1), channel_id=1, source_target_pairs={{0,4},{8,12},{16,20},{24,28},{32,36},{40,44},{48,52},{56,60},{64,6... | collective-permute-start | bytes 983048 | tf_op jit(solution)/shard_map/ppermute | solution.py:41
  18.2 18.9 %collective-permute-start.3 = (bf16[26,128,128]{2,1,0:T(8,128)(2,1)S(1)}, bf16[26,128,128]{2,1,0:T(8,128)(2,1)S(1)}, u32[]{:S(2)}, u32[]{:S(2)}) collective-permute-start(bf16[26,128,128]{2,1,0:T(8,128)(2,1)S(1)} %get-tuple-element.26), channel_id=1, source_target_pairs={{0,1},{1,2},{2,3},{4,5},{5,6},{6,7},{8,9},{9,10},{10,11},{12,13},{... | collective-permute-start | bytes 2555912 | tf_op jit(solution)/shard_map/ppermute | solution.py:41
  22.4 20.1 %collective-permute-start.7 = (bf16[12,128,128]{2,1,0:T(8,128)(2,1)S(1)}, bf16[12,128,128]{2,1,0:T(8,128)(2,1)S(1)}, u32[]{:S(2)}, u32[]{:S(2)}) collective-permute-start(bf16[12,128,128]{2,1,0:T(8,128)(2,1)S(1)} %sent_0.1._), channel_id=1, source_target_pairs={{0,8},{1,9},{2,10},{3,11},{4,12},{5,13},{6,14},{7,15},{8,16},{9,17... | collective-permute-start | bytes 1179656 | tf_op jit(solution)/shard_map/ppermute | solution.py:41
  37.8 13.3 %collective-permute-start.6 = (bf16[6,128,128]{2,1,0:T(8,128)(2,1)S(1)}, bf16[6,128,128]{2,1,0:T(8,128)(2,1)S(1)}, u32[]{:S(2)}, u32[]{:S(2)}) collective-permute-start(bf16[6,128,128]{2,1,0:T(8,128)(2,1)S(1)} %sent_12.1._), channel_id=1, source_target_pairs={{0,8},{1,9},{2,10},{3,11},{4,12},{5,13},{6,14},{7,15},{8,16},{9,17... | collective-permute-start | bytes 589832 | tf_op jit(solution)/shard_map/ppermute | solution.py:41
  39.9 21.5 %collective-permute-start.5 = (bf16[6,128,128]{2,1,0:T(8,128)(2,1)S(1)}, bf16[6,128,128]{2,1,0:T(8,128)(2,1)S(1)}, u32[]{:S(2)}, u32[]{:S(2)}) collective-permute-start(bf16[6,128,128]{2,1,0:T(8,128)(2,1)S(1)} %sent_18.1._), channel_id=1, source_target_pairs={{0,8},{1,9},{2,10},{3,11},{4,12},{5,13},{6,14},{7,15},{8,16},{9,17... | collective-permute-start | bytes 589832 | tf_op jit(solution)/shard_map/ppermute | solution.py:41
  42.7 20.7 %collective-permute-start.10 = (bf16[12,128,128]{2,1,0:T(8,128)(2,1)S(1)}, bf16[12,128,128]{2,1,0:T(8,128)(2,1)S(1)}, u32[]{:S(2)}, u32[]{:S(2)}) collective-permute-start(bf16[12,128,128]{2,1,0:T(8,128)(2,1)S(1)} %total_0.1.refs_1_.done_ref), channel_id=1, source_target_pairs={{0,64},{64,128},{128,192},{192,256},{256,320},{320,384},{384,448},... | collective-permute-start | bytes 1179656 | tf_op jit(solution)/shard_map/ppermute | solution.py:41
  51.1 13.2 %collective-permute-start.9 = (bf16[6,128,128]{2,1,0:T(8,128)(2,1)S(1)}, bf16[6,128,128]{2,1,0:T(8,128)(2,1)S(1)}, u32[]{:S(2)}, u32[]{:S(2)}) collective-permute-start(bf16[6,128,128]{2,1,0:T(8,128)(2,1)S(1)} %total_12.1.refs_1_.done_ref), channel_id=1, source_target_pairs={{0,64},{64,128},{128,192},{192,256},{256,320},{320,384},{384,448},... | collective-permute-start | bytes 589832 | tf_op jit(solution)/shard_map/ppermute | solution.py:41
  61.5 7.0 %collective-permute-start.8 = (bf16[6,128,128]{2,1,0:T(8,128)(2,1)S(1)}, bf16[6,128,128]{2,1,0:T(8,128)(2,1)S(1)}, u32[]{:S(2)}, u32[]{:S(2)}) collective-permute-start(bf16[6,128,128]{2,1,0:T(8,128)(2,1)S(1)} %total_18.1.done_ref), channel_id=1, source_target_pairs={{0,64},{64,128},{128,192},{192,256},{256,320},{320,384},{384,448},... | collective-permute-start | bytes 589832 | tf_op jit(solution)/shard_map/ppermute | solution.py:41
